TPU v7x, 32 devices: a whole 2x2x4 slice. The times are simulated.
32 devices in a mesh: ens: 2 (over y), wide: 4 (over z), lev: 2 (over x), fld: 2 (over core).
Axes of the slice: x: 2, y: 2, z: 4, core: 2. Of those that a mesh axis runs over, the one named last changes fastest.
Arguments:
- fourier_input_rows: bfloat16 [4, 1280, 4, 4, 256], P('ens', 'wide', None, 'fld', 'lev'), parts along dimension 0, may hold values from -6 to 6
- legendre: bfloat16 [4, 1280, 1280], P('wide', ('lev', 'fld')), may hold values from -0.15625 to 0.15625
- slot_wave: int32 [4], P('wide'), may hold values from 0 to 1279, as said below
- to_modes: bfloat16 [128, 128], replicated, may hold values from -0.5 to 0.5
- from_modes: bfloat16 [128, 128], replicated, may hold values from -0.5 to 0.5
- mode_rate: float32 [128], replicated, may hold values from 0.05 to 5
Outputs:
- fourier_out: bfloat16 [4, 1280, 4, 4, 256], P('ens', 'wide', None, 'fld', 'lev'), parts along dimension 0
- spectral: bfloat16 [8, 1280, 4, 256], P(('ens', 'wide'), None, 'fld', 'lev'), parts along dimension 0
There are 2 independent parts, one for each index of `ens`. A program takes and returns all parts, laid end to end along the dimension named above; an argument that names none is the same for every part. Nothing has to cross between parts.
Inputs may be any that keep to these rules, and one draw needn't show every extreme that they name: `slot_wave`: the wavenumbers of the slots are distinct; one slot holds 0 and one holds 1279.
All inputs are finite; a program needn't handle non-finite values.
Results may differ from a plain program's by a relative error of at most 0.0065.
Values may be sent and summed in bfloat16 or wider, within the bound.
No kernel may reach another device: no remote copies, remote signals or barrier semaphores. Data moves between devices by JAX's collectives and lax.ppermute only.
A program may use at most 64 MiB of HBM per device.

v0:
```python
import math

import jax
import jax.numpy as jnp
from jax import lax
from jax.sharding import PartitionSpec as P


def latitude_weights(count):
    position = jnp.arange(count, dtype=jnp.float32)
    return jnp.sin(math.pi * (position + 0.5) / (2 * count))


def project(level_grid, degree_real, weight_rows, rate_rows, degree_total):
    projected = jnp.einsum(
        "kl,snflr->snfkr", weight_rows, level_grid, preferred_element_type=jnp.float32
    )
    factor = 1.0 + degree_real[:, None] * (degree_real[:, None] + 1.0) * rate_rows[None, :] / (
        degree_total * degree_total
    )
    return (projected / factor[None, :, None, :, None]).astype(jnp.bfloat16)


def shards(fourier_input_rows, legendre, slot_wave, to_modes, from_modes, mode_rate):
    wave_rows = lax.all_to_all(fourier_input_rows, "wide", split_axis=2, concat_axis=1, tiled=True)
    half_count = wave_rows.shape[1]
    slot_count = wave_rows.shape[2]
    field_count = wave_rows.shape[3]
    column_count = wave_rows.shape[4]
    degree_count = legendre.shape[1] * lax.axis_size(("lev", "fld"))
    weights = latitude_weights(half_count)[:, None, None, None]
    north_half = wave_rows[0].astype(jnp.float32)
    south_half = wave_rows[1].astype(jnp.float32)
    symmetric = (weights * (north_half + south_half)).astype(jnp.bfloat16)
    antisym = (weights * (north_half - south_half)).astype(jnp.bfloat16)
    paired = jnp.concatenate((symmetric, antisym), axis=3)

    def direct_rows(section, first_row):
        row_count = section.shape[1]
        degree = first_row + jnp.arange(row_count, dtype=jnp.int32)
        relative = degree[None, :] - slot_wave[:, None]
        product = jnp.einsum("snj,jsfc->snfc", section, paired, preferred_element_type=jnp.float32)
        is_even = (relative % 2 == 0)[:, :, None, None]
        is_live = (relative >= 0)[:, :, None, None]
        picked = jnp.where(is_even, product[..., :column_count], product[..., column_count:])
        return jnp.where(is_live, picked, jnp.zeros_like(picked))

    full_table = lax.all_gather(legendre, ("lev", "fld"), axis=1, tiled=True)
    block_rows = 128
    block_count = degree_count // block_rows

    def direct_step(block_index, buffer):
        first_row = block_index * block_rows
        section = lax.dynamic_slice_in_dim(full_table, first_row, block_rows, 1)
        result = direct_rows(section, first_row).astype(jnp.bfloat16)
        return lax.dynamic_update_slice_in_dim(buffer, result, first_row, 1)

    initial_raw = jnp.zeros((slot_count, degree_count, field_count, column_count), jnp.bfloat16)
    raw_spectral = lax.fori_loop(0, block_count, direct_step, initial_raw)
    own_levels = column_count // 2
    first_level = lax.axis_index("lev") * own_levels
    degree_real = jnp.arange(degree_count, dtype=jnp.float32)
    all_levels = lax.all_gather(raw_spectral, "lev", axis=3, tiled=True)
    level_count = all_levels.shape[3] // 2
    level_grid = all_levels.reshape(slot_count, degree_count, field_count, level_count, 2)
    weight_rows = lax.dynamic_slice_in_dim(to_modes, first_level, own_levels, 0)
    rate_rows = lax.dynamic_slice_in_dim(mode_rate, first_level, own_levels, 0)
    own_modes = project(level_grid, degree_real, weight_rows, rate_rows, degree_count).reshape(
        slot_count, degree_count, field_count, column_count
    )
    mode_values = lax.all_gather(own_modes, "lev", axis=3, tiled=True).reshape(
        slot_count, degree_count, field_count, level_count, 2
    )
    back_rows = lax.dynamic_slice_in_dim(from_modes, first_level, own_levels, 0)
    spectral = jnp.einsum(
        "lk,snfkr->snflr", back_rows, mode_values, preferred_element_type=jnp.float32
    )
    spectral = spectral.astype(jnp.bfloat16).reshape(
        slot_count, degree_count, field_count, column_count
    )

    def inverse_rows(running, section, first_row):
        row_count = section.shape[1]
        degree = first_row + jnp.arange(row_count, dtype=jnp.int32)
        relative = degree[None, :] - slot_wave[:, None]
        spec_rows = lax.dynamic_slice_in_dim(spectral, first_row, row_count, 1)
        even_mask = ((relative >= 0) & (relative % 2 == 0))[:, :, None, None]
        odd_mask = ((relative >= 0) & (relative % 2 == 1))[:, :, None, None]
        empty_rows = jnp.zeros_like(spec_rows)
        parity_split = jnp.concatenate(
            (
                jnp.where(even_mask, spec_rows, empty_rows),
                jnp.where(odd_mask, spec_rows, empty_rows),
            ),
            axis=3,
        )
        return running + jnp.einsum(
            "snj,snfc->jsfc", section, parity_split, preferred_element_type=jnp.float32
        )

    initial_sum = jnp.zeros((half_count, slot_count, field_count, 2 * column_count), jnp.float32)

    def inverse_step(block_index, running):
        first_row = block_index * block_rows
        section = lax.dynamic_slice_in_dim(full_table, first_row, block_rows, 1)
        return inverse_rows(running, section, first_row)

    running = lax.fori_loop(0, block_count, inverse_step, initial_sum)
    even_sum = running[..., :column_count]
    odd_sum = running[..., column_count:]
    fourier_wave = jnp.stack((even_sum + odd_sum, even_sum - odd_sum), axis=0).astype(jnp.bfloat16)
    fourier_out = lax.all_to_all(fourier_wave, "wide", split_axis=1, concat_axis=2, tiled=True)
    return (fourier_out, spectral)


def solution(mesh):
    in_specs = (
        P("ens", "wide", None, "fld", "lev"),
        P("wide", ("lev", "fld"), None),
        P("wide"),
        P(),
        P(),
        P(),
    )
    out_specs = (P("ens", "wide", None, "fld", "lev"), P(("ens", "wide"), None, "fld", "lev"))
    return jax.shard_map(shards, mesh=mesh, in_specs=in_specs, out_specs=out_specs, check_vma=False)
```

profile of v0, /device:TPU:0, one launch (start us, length us, event | category | flops | bytes accessed | tf_op | source)
XLA Modules:
  0.0 206.5 jit_solution(15960541568794821746)
XLA Ops:
  7.2 0.7 all-gather.4.cloned.1.call-update
  7.9 3.3 %copy.24 = bf16[2,320,4,2,128]{4,3,1,0,2:T(2,128)(2,1)} copy(bf16[2,320,4,2,128]{4,3,2,1,0:T(2,128)(2,1)} %param.10) | data formatting | bytes 2621440 | tf_op args[0]
  11.2 6.3 %all-to-all-start = ((bf16[2,320,4,2,128]{4,3,1,0,2:T(2,128)(2,1)}), bf16[2,320,4,2,128]{4,3,1,0,2:T(2,128)(2,1)S(1)}, u32[]{:S(2)}, u32[]{:S(2)}) async-start(bf16[2,320,4,2,128]{4,3,1,0,2:T(2,128)(2,1)} %copy.24), calls=%async_computation | async-start | bytes 2621440 | tf_op jit(solution)/shard_map/all_to_all | solution.py:25
  17.6 31.3 %all-to-all-done = bf16[2,320,4,2,128]{4,3,1,0,2:T(2,128)(2,1)S(1)} async-done(((bf16[2,320,4,2,128]{4,3,1,0,2:T(2,128)(2,1)}), bf16[2,320,4,2,128]{4,3,1,0,2:T(2,128)(2,1)S(1)}, u32[]{:S(2)}, u32[]{:S(2)}) %all-to-all-start) | async-done | bytes 1310752 | tf_op jit(solution)/shard_map/all_to_all | solution.py:25
  48.8 0.9 convert_add_fusion
  50.3 21.4 %while.31 = (s32[]{:T(128)}, bf16[1,1280,2,128]{3,1,2,0:T(8,128)(2,1)S(1)}, s32[1]{0:T(128)}, bf16[1,1280,1280]{2,1,0:T(8,128)(2,1)}, bf16[1280,1,2,256]{3,0,2,1...) while((s32[]{:T(128)}, bf16[1,1280,2,128]{3,1,2,0:T(8,128)(2,1)S(1)}, s32[1]{0:T(128)}, ...), condition=%wide.region_1.2_spmd, body=%wide.region_0.1_spmd.sunk | while | flops 167839616 | bytes 1967515 | solution.py:59
  50.4 1.3 fusion.47
  52.5 1.3 fusion.47
  54.6 1.3 fusion.47
  56.8 1.3 fusion.47
  58.9 1.3 fusion.47
  61.1 1.3 fusion.47
  63.2 1.3 fusion.47
  65.3 1.3 fusion.47
  67.5 1.3 fusion.47
  69.6 1.3 fusion.47
  71.8 0.8 copy-done.1
  72.9 23.2 %all-gather.6.cloned.1.call-done = bf16[1,1280,2,256]{3,1,2,0:T(8,128)(2,1)} async-done(((bf16[1,1280,2,128]{3,1,2,0:T(8,128)(2,1)}), bf16[1,1280,2,256]{3,1,2,0:T(8,128)(2,1)}) %all-gather.6.cloned.1.call-update) | async-done | bytes 1310736 | tf_op jit(solution)/shard_map/all_gather | solution.py:63
  96.1 3.6 %copy.27 = bf16[1,1280,2,256]{1,2,3,0:T(2,128)(2,1)S(1)} copy(bf16[1,1280,2,256]{3,1,2,0:T(8,128)(2,1)} %all-gather.6.cloned.1.call-done) | data formatting | bytes 2621440 | tf_op jit(solution)/shard_map/all_gather | solution.py:63
  100.1 1.5 copy.29
  101.6 24.4 %all-gather.8.cloned.1.call-done = bf16[1,1280,2,256]{1,2,0,3:T(2,128)(2,1)} async-done(((bf16[1,1280,2,128]{1,2,0,3:T(2,128)(2,1)}), bf16[1,1280,2,256]{1,2,0,3:T(2,128)(2,1)}) %all-gather.8.cloned.1.call-update) | async-done | bytes 1310736 | tf_op jit(solution)/shard_map/all_gather | solution.py:71
  126.0 1.6 fusion.22
  127.7 0.7 copy.32
  128.4 25.0 %while.32 = (s32[]{:T(128)}, f32[1280,1,2,256]{0,3,2,1:T(8,128)S(1)}, s32[1]{0:T(128)}, bf16[1,1280,2,128]{1,2,3,0:T(2,128)(2,1)S(1)}, bf16[1,1280,1280]{2,1,0:T...) while((s32[]{:T(128)}, f32[1280,1,2,256]{0,3,2,1:T(8,128)S(1)}, s32[1]{0:T(128)}, ...), condition=%wide.region_3.4_spmd.clone, body=%wide.region_2.3_spmd.clone.sunk | while | flops 169412864 | bytes 6029989 | solution.py:108
  128.4 0.7 compare_and_fusion.3
  129.1 1.7 fusion.51
  130.9 0.7 compare_and_fusion.3
  131.6 1.7 fusion.51
  133.4 0.7 compare_and_fusion.3
  134.1 1.7 fusion.51
  135.9 0.7 compare_and_fusion.3
  136.6 1.7 fusion.51
  138.4 0.7 compare_and_fusion.3
  139.1 1.7 fusion.51
  140.9 0.7 compare_and_fusion.3
  141.6 1.7 fusion.51
  144.1 1.7 fusion.51
  145.9 0.7 compare_and_fusion.3
  146.6 1.7 fusion.51
  149.1 1.7 fusion.51
  151.6 1.7 fusion.51
  153.4 3.1 %copy.34 = f32[1280,1,2,256]{3,2,0,1:T(2,128)} copy(f32[1280,1,2,256]{0,3,2,1:T(8,128)S(1)} %get-tuple-element.269) | data formatting | bytes 5242880 | tf_op jit(solution)/shard_map/while | solution.py:108
  156.5 2.2 %fusion.30 = (bf16[1,1280,1,2,128]{4,3,0,2,1:T(2,128)(2,1)S(1)}, bf16[1,1280,1,2,128]{4,3,0,2,1:T(2,128)(2,1)S(1)}) fusion(f32[1280,1,2,256]{3,2,0,1:T(2,128)} %copy.34), kind=kLoop, calls=%fused_computation.54 | loop fusion | flops 1310720 | bytes 3932160 | tf_op jit(solution)/shard_map/stack | solution.py:111
  158.7 2.7 %pad_maximum_fusion.1 = bf16[2,1280,1,2,128]{4,3,0,2,1:T(2,128)(2,1)} fusion(bf16[1,1280,1,2,128]{4,3,0,2,1:T(2,128)(2,1)S(1)} %get-tuple-element.334, bf16[1,1280,1,2,128]{4,3,0,2,1:T(2,128)(2,1)S(1)} %get-tuple-element.333), kind=kLoop, calls=%fused_computation.45 | loop fusion | flops 655360 | bytes 2621440 | tf_op jit(solution)/shard_map/stack | solution.py:111
  161.5 4.6 %all-to-all-start.1 = ((bf16[2,1280,1,2,128]{4,3,0,2,1:T(2,128)(2,1)}), bf16[2,1280,1,2,128]{4,3,0,2,1:T(2,128)(2,1)S(1)}, u32[]{:S(2)}, u32[]{:S(2)}) async-start(bf16[2,1280,1,2,128]{4,3,0,2,1:T(2,128)(2,1)} %pad_maximum_fusion.1), calls=%async_computation.1 | async-start | bytes 2621440 | tf_op jit(solution)/shard_map/all_to_all | solution.py:112
  166.1 2.1 %copy.39 = bf16[1,1280,2,128]{3,2,1,0:T(2,128)(2,1)} copy(bf16[1,1280,2,128]{1,2,3,0:T(2,128)(2,1)S(1)} %get-tuple-element.472) | data formatting | bytes 1310720
  168.2 29.2 %all-to-all-done.1 = bf16[2,1280,1,2,128]{4,3,0,2,1:T(2,128)(2,1)S(1)} async-done(((bf16[2,1280,1,2,128]{4,3,0,2,1:T(2,128)(2,1)}), bf16[2,1280,1,2,128]{4,3,0,2,1:T(2,128)(2,1)S(1)}, u32[]{:S(2)}, u32[]{:S(2)}) %all-to-all-start.1) | async-done | bytes 1310752 | tf_op jit(solution)/shard_map/all_to_all | solution.py:112
  197.6 2.4 %copy.38 = bf16[2,320,4,2,128]{4,3,2,1,0:T(2,128)(2,1)} copy(bf16[2,320,4,2,128]{4,1,2,3,0:T(8,128)(2,1)S(1)} %bitcast.88) | data formatting | bytes 2621440
  (66 shorter events, 12.0 us)
Async XLA Ops:
  7.2 92.5 %copy-start = (bf16[128,128]{1,0:T(8,128)(2,1)S(1)}, bf16[128,128]{1,0:T(8,128)(2,1)}, u32[]{:S(2)}) copy-start(bf16[128,128]{1,0:T(8,128)(2,1)} %param.13) | copy-start | bytes 98308
  7.2 43.1 %all-gather.4.cloned.1.call-start = ((), (), s32[]{:S(2)}) async-start(), calls=%async_computation.2 | async-start | bytes 4096000 | tf_op jit(solution)/shard_map/all_gather | solution.py:48
  11.2 37.7 %all-to-all-start = ((bf16[2,320,4,2,128]{4,3,1,0,2:T(2,128)(2,1)}), bf16[2,320,4,2,128]{4,3,1,0,2:T(2,128)(2,1)S(1)}, u32[]{:S(2)}, u32[]{:S(2)}) async-start(bf16[2,320,4,2,128]{4,3,1,0,2:T(2,128)(2,1)} %copy.24), calls=%async_computation | async-start | bytes 2621440 | tf_op jit(solution)/shard_map/all_to_all | solution.py:25
  17.5 78.6 %all-gather.6.cloned.1.call-start = ((), (), s32[]{:S(2)}) async-start(), calls=%async_computation.3 | async-start | bytes 1966080 | tf_op jit(solution)/shard_map/all_gather | solution.py:63
  50.3 22.3 %copy-start.3 = (f32[128]{0:T(128)S(1)}, f32[128]{0:T(128)}, u32[]{:S(2)}) copy-start(f32[128]{0:T(128)} %param.15) | copy-start | bytes 1540
  71.7 0.8 copy-start.1
  72.6 53.4 %all-gather.8.cloned.1.call-start = ((), (), s32[]{:S(2)}) async-start(), calls=%async_computation.4 | async-start | bytes 1966080 | tf_op jit(solution)/shard_map/all_gather | solution.py:71
  100.1 26.0 %copy-start.2 = (bf16[128,128]{1,0:T(8,128)(2,1)S(1)}, bf16[128,128]{1,0:T(8,128)(2,1)}, u32[]{:S(2)}) copy-start(bf16[128,128]{1,0:T(8,128)(2,1)} %param.14) | copy-start | bytes 98308
  161.5 35.9 %all-to-all-start.1 = ((bf16[2,1280,1,2,128]{4,3,0,2,1:T(2,128)(2,1)}), bf16[2,1280,1,2,128]{4,3,0,2,1:T(2,128)(2,1)S(1)}, u32[]{:S(2)}, u32[]{:S(2)}) async-start(bf16[2,1280,1,2,128]{4,3,0,2,1:T(2,128)(2,1)} %pad_maximum_fusion.1), calls=%async_computation.1 | async-start | bytes 2621440 | tf_op jit(solution)/shard_map/all_to_all | solution.py:112
Sparse Core Ops, SparseCore 0:
  9.6 31.9 all-gather.3
  72.7 23.3 all-gather.5
  101.7 24.2 all-gather.7
where the time goes:
time: 208 us; the launch traced here: 207 us
  waiting for transfers between devices  109 us (52%)
  matrix products  32.3 us (16%)
  other arithmetic  21.1 us (10%)
  local copies, waits for them, and re-layouts  18.4 us (9%)
  between operations  13.9 us (7%)
  starting transfers between devices  11 us (5%)
    all_to_all x1, waiting for transfers between devices, shards(): lax.all_to_all(fourier_input_rows, 'wide', split_axis=2, concat_axis=1, t...  31.3 us
    all_to_all x1, waiting for transfers between devices, shards(): lax.all_to_all(fourier_wave, 'wide', split_axis=1, concat_axis=2, tiled=T...  29.2 us
    all_gather x1, waiting for transfers between devices, shards(): lax.all_gather(own_modes, 'lev', axis=3, tiled=True)  24.4 us
    all_gather x1, waiting for transfers between devices, shards(): all_levels = lax.all_gather(raw_spectral, 'lev', axis=3, tiled=True)  23.2 us
    dot_general x10, matrix products, inverse_rows(): jnp.einsum('snj,snfc->jsfc', section, parity_split, preferred_element_typ...  17.2 us
    dot_general x10, matrix products, direct_rows(): jnp.einsum('snj,jsfc->snfc', section, paired, preferred_element_type=jnp....  13.2 us
    unnamed x11, local copies, waits for them, and re-layouts  8.65 us
    and x10, other arithmetic, inverse_rows(): odd_mask = ((relative >= 0) & (relative % 2 == 1))[:, :, None, None]  6.62 us
  transfers between devices with their start and end apart: 5, of which 4 were waited for; matrix products, arithmetic and copies ran while one was open for 3% of the time, Pallas kernels for 0%

commit v1 on v0

--- a/solution.py
+++ b/solution.py
@@ -1,9 +1,14 @@
+import functools
 import math
 
 import jax
 import jax.numpy as jnp
 from jax import lax
+from jax.experimental import pallas as pl
+from jax.experimental.pallas import tpu as pltpu
 from jax.sharding import PartitionSpec as P
+
+VMEM_BYTES = 8 * 1024 * 1024
 
 
 def latitude_weights(count):
@@ -11,6 +16,339 @@
     return jnp.sin(math.pi * (position + 0.5) / (2 * count))
 
 
+def iota2(shape, dim):
+    return lax.broadcasted_iota(jnp.int32, shape, dim)
+
+
+def picks(condition):
+    return jnp.where(condition, 1.0, 0.0).astype(jnp.bfloat16)
+
+
+def dot32(a, b):
+    return jnp.dot(a, b, preferred_element_type=jnp.float32)
+
+
+def call(body, out_shape, name, flops, scratch=(), scalars=1, after=()):
+    smem = pl.BlockSpec(memory_space=pltpu.SMEM)
+    vmem = pl.BlockSpec(memory_space=pltpu.VMEM)
+
+    def run(*operands):
+        used = len(operands)
+
+        def kernel(*refs):
+            body(*refs[:used], *refs[used + len(after) :])
+
+        return pl.pallas_call(
+            kernel,
+            out_shape=out_shape,
+            in_specs=[smem] * scalars
+            + [vmem] * (used - scalars)
+            + [pl.BlockSpec(memory_space=pl.ANY)] * len(after),
+            out_specs=jax.tree.map(lambda _: vmem, out_shape),
+            scratch_shapes=list(scratch),
+            compiler_params=pltpu.CompilerParams(vmem_limit_bytes=VMEM_BYTES),
+            cost_estimate=pl.CostEstimate(flops=flops, bytes_accessed=0, transcendentals=0),
+            name=name,
+        )(*operands, *after)
+
+    return run
+
+
+def split_body(slots, fields, block, odd, meta_ref, rows_ref, weight_ref, *outs):
+    latitudes = weight_ref.shape[0]
+    group = slots * fields
+    size = block * group
+    out_row, in_row = iota2((size, size), 0), iota2((size, size), 1)
+    pair = out_row // block
+    slot = lax.rem(meta_ref[1] + pair // fields, slots)
+    order = picks(in_row == (out_row % block) * group + slot * fields + pair % fields)
+    for first in range(0, latitudes, block):
+        north = rows_ref[0, first * group : first * group + size, :]
+        south = rows_ref[1, first * group : first * group + size, :]
+        sorted_rows = dot32(order, jnp.concatenate((north, south), axis=1))
+        up, down = sorted_rows[:, :128], sorted_rows[:, 128:]
+        mixed = up - down if odd else up + down
+        weight = weight_ref[first : first + block, :]
+        for shift in range(slots):
+            for field in range(fields):
+                at = (shift * fields + field) * block
+                outs[shift][first : first + block, field * 128 : field * 128 + 128] = (
+                    weight * mixed[at : at + block]
+                ).astype(jnp.bfloat16)
+
+
+def table_body(odd, meta_ref, table_ref, out_ref):
+    rows, columns = table_ref.shape
+    half = rows // 2
+    out_row, in_row = iota2((half, rows), 0), iota2((half, rows), 1)
+    order = picks(in_row == 2 * out_row + (meta_ref[0] + odd) % 2)
+    for first in range(0, columns, 256):
+        lanes = slice(first, first + 256)
+        out_ref[:, lanes] = dot32(order, table_ref[:, lanes]).astype(jnp.bfloat16)
+
+
+def modes_body(flds, degree_total, meta_ref, to_ref, from_ref, rate_ref, in_ref, out_ref, scale_ref):
+    levels = to_ref.shape[0]
+    wide = 2 * levels
+    own = levels // 2
+    lane, row = iota2((levels, wide), 1), iota2((levels, wide), 0)
+    owner = lax.rem(meta_ref[2] + lane // (2 * own), 2)
+    spread = picks(row == owner * own + (lane % (2 * own)) // 2)
+    plain = picks(row == lane // 2)
+    same = (iota2((wide, wide), 0) % 2) == (iota2((wide, wide), 1) % 2)
+
+    def turned(first, matrix, last):
+        half = lax.dot_general(first, matrix, (((0,), (1,)), ((), ())), preferred_element_type=jnp.float32)
+        return jnp.where(same, dot32(half.astype(jnp.bfloat16), last), 0.0).astype(jnp.bfloat16)
+
+    in_ref[...] = turned(spread, to_ref[...], plain)
+    out_ref[...] = turned(plain, from_ref[...], spread)
+    square = (levels, levels)
+    diagonal = jnp.where(iota2(square, 0) == iota2(square, 1), rate_ref[...], 0.0)
+    column = jnp.sum(diagonal, axis=1, keepdims=True)
+    rates = jnp.sum(jnp.where(row == lane // 2, column, 0.0), axis=0, keepdims=True)
+    rows = scale_ref.shape[0] // (2 * flds)
+    for odd in range(2):
+        for g in range(flds):
+            block = (1 - meta_ref[2]) * flds + lax.rem(meta_ref[3] + g, flds)
+            degree = block * (2 * rows) + 2 * iota2((rows, 1), 0) + (meta_ref[0] + odd) % 2
+            real = degree.astype(jnp.float32)
+            factor = 1.0 + real * (real + 1.0) * rates / (degree_total * degree_total)
+            at = (odd * flds + g) * rows
+            scale_ref[at : at + rows, :] = jnp.where(degree >= meta_ref[0], 1.0 / factor, 0.0)
+
+
+def near_body(meta_ref, *refs):
+    parts, tables, (out_ref, data_ref) = refs[:-4], refs[-4:-2], refs[-2:]
+    wide, latitudes = len(parts), parts[0].shape[0]
+    for shift in range(wide):
+        owner = lax.rem(meta_ref[1] - shift + wide, wide)
+        data_ref[pl.ds(pl.multiple_of(owner * latitudes, latitudes), latitudes), :] = parts[shift][...]
+    table = jnp.concatenate([ref[...] for ref in tables], axis=0)
+    out_ref[...] = dot32(table, data_ref[...]).astype(jnp.bfloat16)
+
+
+def far_body(data_ref, first_ref, second_ref, out_ref):
+    table = jnp.concatenate((first_ref[...], second_ref[...]), axis=0)
+    out_ref[...] = dot32(table, data_ref[...]).astype(jnp.bfloat16)
+
+
+def solve_body(odd, own_ref, other_ref, in_ref, out_ref, scale_ref, to_own_ref, to_other_ref):
+    rows, columns = own_ref.shape
+    for lanes in (slice(first, first + 128) for first in range(0, columns, 128)):
+        level_grid = jnp.concatenate((own_ref[:, lanes], other_ref[:, lanes]), axis=1)
+        scale = scale_ref[odd * rows : odd * rows + rows, :]
+        modes = (dot32(level_grid, in_ref[...]) * scale).astype(jnp.bfloat16)
+        result = dot32(modes, out_ref[...]).astype(jnp.bfloat16)
+        to_own_ref[:, lanes] = result[:, :128]
+        to_other_ref[:, lanes] = result[:, 128:]
+
+
+def turned_dot(tables, spectral, chunk):
+    table = jnp.concatenate([ref[:, chunk] for ref in tables], axis=0)
+    return lax.dot_general(table, spectral, (((0,), (0,)), ((), ())), preferred_element_type=jnp.float32)
+
+
+def inverse_far_body(spectral_ref, first_ref, second_ref, out_ref):
+    for first in range(0, out_ref.shape[0], 256):
+        chunk = slice(first, first + 256)
+        out_ref[chunk, :] = turned_dot((first_ref, second_ref), spectral_ref[...], chunk)
+
+
+def inverse_near_body(meta_ref, sum_ref, spectral_ref, first_ref, second_ref, *refs):
+    outs, total = refs[:-1], refs[-1]
+    wide, latitudes = len(outs), outs[0].shape[0]
+    for first in range(0, total.shape[0], 256):
+        chunk = slice(first, first + 256)
+        more = turned_dot((first_ref, second_ref), spectral_ref[...], chunk)
+        total[chunk, :] = (sum_ref[chunk, :] + more).astype(jnp.bfloat16)
+    for shift in range(wide):
+        owner = lax.rem(meta_ref[1] + shift, wide)
+        outs[shift][...] = total[pl.ds(pl.multiple_of(owner * latitudes, latitudes), latitudes), :]
+
+
+def join_body(wide, block, meta_ref, *refs):
+    evens, odds, out_ref = refs[:wide], refs[wide : 2 * wide], refs[2 * wide]
+    latitudes, columns = evens[0].shape
+    fields = columns // 128
+    group = wide * fields
+    size = block * group
+    out_row, in_row = iota2((size, size), 0), iota2((size, size), 1)
+    place = out_row % group
+    shift = lax.rem(meta_ref[1] - place // fields + wide, wide)
+    order = picks(in_row == (shift * fields + place % fields) * block + out_row // group)
+
+    def stack(parts, first):
+        return jnp.concatenate(
+            [
+                part[first : first + block, field * 128 : field * 128 + 128]
+                for part in parts
+                for field in range(fields)
+            ],
+            axis=0,
+        )
+
+    for first in range(0, latitudes, block):
+        both = dot32(order, jnp.concatenate((stack(evens, first), stack(odds, first)), axis=1))
+        even, odd = both[:, :128], both[:, 128:]
+        out_ref[0, first * group : first * group + size, :] = (even + odd).astype(jnp.bfloat16)
+        out_ref[1, first * group : first * group + size, :] = (even - odd).astype(jnp.bfloat16)
+
+
+def rows_body(flds, block, meta_ref, *refs):
+    parts, out_ref = (refs[:2], refs[2:4]), refs[4]
+    total_rows, columns = refs[0].shape
+    rows = total_rows // flds
+    fields = columns // 128
+    group = 2 * fields
+    size = block * group
+    parity = meta_ref[0] % 2
+    out_row, in_row = iota2((size, size), 0), iota2((size, size), 1)
+    place = out_row % group
+    odd = (place // fields + parity) % 2
+    order = picks(in_row == (odd * fields + place % fields) * block + out_row // group)
+    for d in range(2):
+        for g in range(flds):
+            index = lax.rem(meta_ref[2] + d, 2) * flds + lax.rem(meta_ref[3] + g, flds)
+            for first in range(0, rows, block):
+                at = slice(g * rows + first, g * rows + first + block)
+                stacked = jnp.concatenate(
+                    [
+                        part[d][at, field * 128 : field * 128 + 128]
+                        for part in parts
+                        for field in range(fields)
+                    ],
+                    axis=0,
+                )
+                start = pl.multiple_of(index * (rows * group), rows * group) + first * group
+                out_ref[pl.ds(start, size), :] = dot32(order, stacked).astype(jnp.bfloat16)
+
+
+def shards(fourier_input_rows, legendre, slot_wave, to_modes, from_modes, mode_rate):
+    wide, levs, flds = (lax.axis_size(axis) for axis in ("wide", "lev", "fld"))
+    _, latitudes, slots, fields, lanes = fourier_input_rows.shape
+    _, shard_rows, half_count = legendre.shape
+    degree_count = shard_rows * levs * flds
+    columns = fields * lanes
+    group = slots * fields
+    half_rows = shard_rows // 2
+    share = flds * half_rows
+    levels = to_modes.shape[0]
+    block = 256 // group
+    bf16, f32 = jnp.bfloat16, jnp.float32
+
+    def shape(*dims, kind=bf16):
+        return jax.ShapeDtypeStruct(dims, kind)
+
+    def shifted(value, axis, count, step):
+        return lax.ppermute(value, axis, [(i, (i + step) % count) for i in range(count)])
+
+    def across(value, step):
+        return shifted(value, "wide", wide, step)
+
+    def behind(value, *others):
+        return lax.optimization_barrier((value, *others))
+
+    wide_at, lev_at, fld_at = (lax.axis_index(axis) for axis in ("wide", "lev", "fld"))
+    meta = jnp.stack((slot_wave[0], wide_at, lev_at, fld_at)).astype(jnp.int32)
+    position = (wide_at * latitudes + jnp.arange(latitudes, dtype=jnp.int32)).astype(f32)
+    weights = jnp.sin(math.pi * (position + 0.5) / (2 * half_count))
+    weights = jnp.broadcast_to(weights[:, None], (latitudes, lanes))
+    move_flops = 4 * group * latitudes * 128 * 256
+    share_flops = 2 * share * half_count * columns
+
+    def split(odd, after=()):
+        return call(
+            functools.partial(split_body, slots, fields, block, odd), (shape(latitudes, columns),) * wide,
+            "split_hemispheres", move_flops, after=after,
+        )(meta, fourier_input_rows.reshape(2, latitudes * group, lanes), weights)
+
+    def split_table(odd, after):
+        return call(
+            functools.partial(table_body, odd), shape(half_rows, half_count), "split_table",
+            shard_rows * shard_rows * half_count, after=after,
+        )(meta, legendre[0])
+
+    def direct_near(received, table):
+        return call(
+            near_body, (shape(share, columns), shape(half_count, columns)), "direct_legendre_near", share_flops
+        )(meta, *received, *table)
+
+    def direct_far(data, table):
+        return call(far_body, shape(share, columns), "direct_legendre_far", share_flops, scalars=0)(data, *table)
+
+    def solve(odd, own, other):
+        return call(
+            functools.partial(solve_body, odd), (shape(share, columns),) * 2, "vertical_solve",
+            16 * share * fields * levels * levels, scalars=0,
+        )(own, other, *matrices)
+
+    def inverse_far(spectral, table):
+        return call(
+            inverse_far_body, shape(half_count, columns, kind=f32), "inverse_legendre_far", share_flops, scalars=0,
+        )(spectral, *table)
+
+    def inverse_near(total, spectral, table):
+        return call(
+            inverse_near_body, (shape(latitudes, columns),) * wide, "inverse_legendre_near", share_flops,
+            scratch=[pltpu.VMEM((half_count, columns), bf16)],
+        )(meta, total, spectral, *table)
+
+    def over_lev(value):
+        return shifted(value, "lev", levs, 1)
+
+    def beside(value):
+        return shifted(value, "fld", flds, 1)
+
+    even = split(0)
+    even_in = [even[0]] + [across(even[step], step) for step in range(1, wide)]
+    part = split_table(0, (even[0],))
+    even_near, even_far = [part, beside(part)], over_lev(part)
+    even_far, *even_in[1:] = behind(even_far, *even_in[1:])
+    even_far = [even_far, beside(even_far)]
+    odd = split(1, (even_near[1],))
+    odd_part = split_table(1, (odd[0],))
+    *matrices, scale = call(
+        functools.partial(modes_body, flds, degree_count),
+        (shape(2 * levels, 2 * levels),) * 2 + (shape(2 * share, 2 * levels, kind=f32),),
+        "spread_modes", 12 * levels * levels * levels, after=(odd_part,),
+    )(meta, to_modes, from_modes, mode_rate[None, :])
+    matrices = (*matrices, scale)
+
+    odd_in = [odd[0]] + [across(odd[step], step) for step in range(1, wide)]
+    odd_near, odd_far = [odd_part, beside(odd_part)], over_lev(odd_part)
+    odd_far = [odd_far, beside(odd_far)]
+    raw, data = direct_near(even_in, even_near)
+    other, odd_in[2] = behind(over_lev(raw), odd_in[2])
+    to_own, to_other = solve(0, direct_far(data, even_far), other)
+    total = inverse_far(to_own, even_far)
+    from_other, odd_in[1], odd_in[3] = behind(over_lev(to_other), odd_in[1], odd_in[3])
+    even_spectral = [from_other, to_own]
+    grid = inverse_near(total, from_other, even_near)
+
+    even_out = [grid[0]] + [across(grid[step], step) for step in range(1, wide)]
+    raw, data = direct_near(odd_in, odd_near)
+    other, even_out[2] = behind(over_lev(raw), even_out[2])
+    to_own, to_other = solve(1, direct_far(data, odd_far), other)
+    total = inverse_far(to_own, odd_far)
+    from_other, even_out[1], even_out[3] = behind(over_lev(to_other), even_out[1], even_out[3])
+    odd_spectral = [from_other, to_own]
+    grid = inverse_near(total, from_other, odd_near)
+    odd_out = [grid[0]] + [across(grid[step], step) for step in range(1, wide)]
+
+    spectral_rows = call(
+        functools.partial(rows_body, flds, 32), shape(degree_count * fields, lanes), "order_spectral", 0,
+        after=(grid[0],),
+    )(meta, *even_spectral, *odd_spectral)
+    fourier_rows = call(
+        functools.partial(join_body, wide, block), shape(2, latitudes * group, lanes), "join_hemispheres", move_flops,
+    )(meta, *even_out, *odd_out)
+    return (
+        fourier_rows.reshape(2, latitudes, slots, fields, lanes),
+        spectral_rows.reshape(1, degree_count, fields, lanes),
+    )
+
+
 def project(level_grid, degree_real, weight_rows, rate_rows, degree_total):
     projected = jnp.einsum(
         "kl,snflr->snfkr", weight_rows, level_grid, preferred_element_type=jnp.float32
@@ -21,7 +359,7 @@
     return (projected / factor[None, :, None, :, None]).astype(jnp.bfloat16)
 
 
-def shards(fourier_input_rows, legendre, slot_wave, to_modes, from_modes, mode_rate):
+def plain_shards(fourier_input_rows, legendre, slot_wave, to_modes, from_modes, mode_rate):
     wave_rows = lax.all_to_all(fourier_input_rows, "wide", split_axis=2, concat_axis=1, tiled=True)
     half_count = wave_rows.shape[1]
     slot_count = wave_rows.shape[2]
@@ -123,4 +461,19 @@
         P(),
     )
     out_specs = (P("ens", "wide", None, "fld", "lev"), P(("ens", "wide"), None, "fld", "lev"))
-    return jax.shard_map(shards, mesh=mesh, in_specs=in_specs, out_specs=out_specs, check_vma=False)
+
+    def body(fourier_input_rows, legendre, *rest):
+        _, latitudes, slots, fields, lanes = fourier_input_rows.shape
+        whole_tiles = (
+            latitudes % 32 == 0
+            and fields == 2
+            and slots == mesh.shape["wide"] == 4
+            and mesh.shape["ens"] == mesh.shape["lev"] == mesh.shape["fld"] == 2
+            and lanes == 128
+            and legendre.shape[1] % 64 == 0
+            and legendre.shape[2] % 256 == 0
+        )
+        form = shards if whole_tiles else plain_shards
+        return form(fourier_input_rows, legendre, *rest)
+
+    return jax.shard_map(body, mesh=mesh, in_specs=in_specs, out_specs=out_specs, check_vma=False)

time: 208 us -> 85.2 us (0.41)
  waiting for transfers between devices: 109 us -> 30.2 us
  matrix products: 32.3 us -> 0 us
  starting transfers between devices: 11 us -> 34.7 us
  other arithmetic: 21.1 us -> 0.12 us
  Pallas kernels: 0 us -> 15.9 us
  local copies, waits for them, and re-layouts: 18.4 us -> 2.58 us
  between operations: 13.9 us -> 1.5 us
    all_to_all x2 -> x0, waiting for transfers between devices: 60.5 us -> none  [the longest x1 31.3 us: shards(): lax.all_to_all(fourier_input_rows, 'wide', split_axis=2, concat_axis=1, t...]
    all_gather x3 -> x0, waiting for transfers between devices: 47.7 us -> none  [the longest x1 24.4 us: shards(): lax.all_gather(own_modes, 'lev', axis=3, tiled=True)]
    ppermute x0 -> x22, starting transfers between devices: none -> 34.7 us  [shifted(): lax.ppermute(value, axis, [(i, (i + step) % count) for i in range(count)])]
    dot_general x22 -> x0, matrix products: 32.3 us -> none  [the longest x10 17.2 us: inverse_rows(): jnp.einsum('snj,snfc->jsfc', section, parity_split, preferred_element_typ...]
    ppermute x0 -> x22, waiting for transfers between devices: none -> 30.2 us  [shifted(): lax.ppermute(value, axis, [(i, (i + step) % count) for i in range(count)])]
    pallas_call x0 -> x17, Pallas kernels: none -> 15.9 us  [run(): pl.pallas_call(kernel, out_shape=out_shape, in_specs=[smem] * scalars + [...]
    all_to_all x2 -> x0, starting transfers between devices: 10.9 us -> none  [the longest x1 6.32 us: shards(): lax.all_to_all(fourier_input_rows, 'wide', split_axis=2, concat_axis=1, t...]
    and x10 -> x0, other arithmetic: 6.62 us -> none  [inverse_rows(): odd_mask = ((relative >= 0) & (relative % 2 == 1))[:, :, None, None]]
  transfers between devices with their start and end apart: 5 -> 22, of which waited for: 4 -> 10; matrix products, arithmetic and copies ran while one was open for 3% -> 0% of each run, Pallas kernels for 0% -> 12%
where the time goes in v1:
time: 85.2 us; the launch traced here: 85 us
  starting transfers between devices  34.7 us (41%)
  waiting for transfers between devices  30.2 us (35%)
  Pallas kernels  15.9 us (19%)
  local copies, waits for them, and re-layouts  2.58 us (3%)
  between operations  1.5 us (2%)
    ppermute x22, starting transfers between devices, shifted(): lax.ppermute(value, axis, [(i, (i + step) % count) for i in range(count)])  34.7 us
    ppermute x22, waiting for transfers between devices, shifted(): lax.ppermute(value, axis, [(i, (i + step) % count) for i in range(count)])  30.2 us
    pallas_call x17, Pallas kernels, run(): pl.pallas_call(kernel, out_shape=out_shape, in_specs=[smem] * scalars + [...  15.9 us
    unnamed x12, local copies, waits for them, and re-layouts  2.48 us
  transfers between devices with their start and end apart: 22, of which 10 were waited for; matrix products, arithmetic and copies ran while one was open for 0% of the time, Pallas kernels for 12%

profile of v1, /device:TPU:0, one launch (start us, length us, event | category | flops | bytes accessed | tf_op | source)
XLA Modules:
  0.0 85.0 jit_solution(8262153933548785177)
XLA Ops:
  1.4 0.1 broadcast_in_dim.4.refs_2_
  1.5 1.3 %copy-done = bf16[2,320,4,2,128]{4,3,2,1,0:T(2,128)(2,1)S(1)} copy-done((bf16[2,320,4,2,128]{4,3,2,1,0:T(2,128)(2,1)S(1)}, bf16[2,320,4,2,128]{4,3,2,1,0:T(2,128)(2,1)}, u32[]{:S(2)}) %copy-start) | copy-done | bytes 1310744
  2.8 1.1 %split_hemispheres.2 = (bf16[320,256]{1,0:T(8,128)(2,1)S(1)}, bf16[320,256]{1,0:T(8,128)(2,1)S(1)}, bf16[320,256]{1,0:T(8,128)(2,1)S(1)}, bf16[320,256]{1,0:T(8,128)(2,1)S(1)}) custom-call(s32[4]{0:T(128)S(1)} %pad_add_fusion.refs_0_, bf16[2,2560,128]{2,1,0:T(8,128)(2,1)S(1)} %bitcast.8, f32[320,128]{1,0:T(8,128)S(1)} %broadcast_in_dim.4.refs_2_), custom_call_target="tpu_custom_call" | custom-call | flops 335544320 | tf_op jit(solution)/shard_map/split_hemispheres/pallas_call | solution.py:41
  3.9 1.1 %copy-done.2 = bf16[1,320,1280]{2,1,0:T(8,128)(2,1)S(1)} copy-done((bf16[1,320,1280]{2,1,0:T(8,128)(2,1)S(1)}, bf16[1,320,1280]{2,1,0:T(8,128)(2,1)}, u32[]{:S(2)}) %copy-start.2) | copy-done | bytes 819224
  5.1 0.9 %split_table.2.refs_5_.refs_3_ = bf16[160,1280]{1,0:T(8,128)(2,1)S(1)} custom-call(s32[4]{0:T(128)S(1)} %pad_add_fusion.refs_0_, bf16[320,1280]{1,0:T(8,128)(2,1)S(1)} %bitcast.10, bf16[320,256]{1,0:T(8,128)(2,1)S(1)} %get-tuple-element.43.refs_2_.refs_1_), custom_call_target="tpu_custom_call" | custom-call | flops 131072000 | tf_op jit(solution)/shard_map/split_table/pallas_call | solution.py:41
  6.0 0.5 collective-permute-start.4
  6.5 2.6 %collective-permute-start = (bf16[160,1280]{1,0:T(8,128)(2,1)S(1)}, bf16[160,1280]{1,0:T(8,128)(2,1)S(1)}, u32[]{:S(2)}, u32[]{:S(2)}) collective-permute-start(bf16[160,1280]{1,0:T(8,128)(2,1)S(1)} %split_table.2.refs_5_.refs_3_), channel_id=1, source_target_pairs={{0,2},{2,0},{1,3},{3,1},{4,6},{6,4},{5,7},{7,5},{8,10},{10,8},{9,1... | collective-permute-start | bytes 1228808 | tf_op jit(solution)/shard_map/ppermute | solution.py:244
  9.1 1.6 %collective-permute-start.1 = (bf16[320,256]{1,0:T(8,128)(2,1)S(1)}, bf16[320,256]{1,0:T(8,128)(2,1)S(1)}, u32[]{:S(2)}, u32[]{:S(2)}) collective-permute-start(bf16[320,256]{1,0:T(8,128)(2,1)S(1)} %get-tuple-element.44), channel_id=1, source_target_pairs={{0,4},{4,8},{8,12},{12,0},{1,5},{5,9},{9,13},{13,1},{2,6},{6,10},{... | collective-permute-start | bytes 491528 | tf_op jit(solution)/shard_map/ppermute | solution.py:244
  10.6 2.6 %collective-permute-start.2 = (bf16[320,256]{1,0:T(8,128)(2,1)S(1)}, bf16[320,256]{1,0:T(8,128)(2,1)S(1)}, u32[]{:S(2)}, u32[]{:S(2)}) collective-permute-start(bf16[320,256]{1,0:T(8,128)(2,1)S(1)} %get-tuple-element.45), channel_id=1, source_target_pairs={{0,8},{4,12},{8,0},{12,4},{1,9},{5,13},{9,1},{13,5},{2,10},{6,14},... | collective-permute-start | bytes 491528 | tf_op jit(solution)/shard_map/ppermute | solution.py:244
  13.2 1.3 %collective-permute-start.3 = (bf16[320,256]{1,0:T(8,128)(2,1)S(1)}, bf16[320,256]{1,0:T(8,128)(2,1)S(1)}, u32[]{:S(2)}, u32[]{:S(2)}) collective-permute-start(bf16[320,256]{1,0:T(8,128)(2,1)S(1)} %get-tuple-element.46), channel_id=1, source_target_pairs={{0,12},{4,0},{8,4},{12,8},{1,13},{5,1},{9,5},{13,9},{2,14},{6,2},{... | collective-permute-start | bytes 491528 | tf_op jit(solution)/shard_map/ppermute | solution.py:244
  14.6 1.1 %split_hemispheres.3 = (bf16[320,256]{1,0:T(8,128)(2,1)S(1)}, bf16[320,256]{1,0:T(8,128)(2,1)S(1)}, bf16[320,256]{1,0:T(8,128)(2,1)S(1)}, bf16[320,256]{1,0:T(8,128)(2,1)S(1)}) custom-call(s32[4]{0:T(128)S(1)} %pad_add_fusion.refs_0_, bf16[2,2560,128]{2,1,0:T(8,128)(2,1)S(1)} %bitcast.9, f32[320,128]{1,0:T(8,128)S(1)} %broadcast_in_dim.4.refs_2_, ...), custom_call_target="tpu_custom_call" | custom-call | flops 335544320 | tf_op jit(solution)/shard_map/split_hemispheres/pallas_call | solution.py:41
  15.7 0.9 %split_table.3.refs_4_.refs_5_.refs_3_ = bf16[160,1280]{1,0:T(8,128)(2,1)S(1)} custom-call(s32[4]{0:T(128)S(1)} %pad_add_fusion.refs_0_, bf16[320,1280]{1,0:T(8,128)(2,1)S(1)} %bitcast.11, bf16[320,256]{1,0:T(8,128)(2,1)S(1)} %get-tuple-element.55.refs_2_.refs_1_), custom_call_target="tpu_custom_call" | custom-call | flops 131072000 | tf_op jit(solution)/shard_map/split_table/pallas_call | solution.py:41
  16.6 0.6 collective-permute-start.12
  17.2 0.8 collective-permute-done.1.refs_2_
  18.0 6.3 %collective-permute-done.2.refs_3_ = bf16[320,256]{1,0:T(8,128)(2,1)S(1)} collective-permute-done((bf16[320,256]{1,0:T(8,128)(2,1)S(1)}, bf16[320,256]{1,0:T(8,128)(2,1)S(1)}, u32[]{:S(2)}, u32[]{:S(2)}) %collective-permute-start.2) | collective-permute-done | bytes 163872 | tf_op jit(solution)/shard_map/ppermute | solution.py:244
  24.3 0.5 collective-permute-start.11
  24.8 1.0 %direct_legendre_near.2 = (bf16[320,256]{1,0:T(8,128)(2,1)S(1)}, bf16[1280,256]{1,0:T(8,128)(2,1)S(1)}) custom-call(s32[4]{0:T(128)S(1)} %pad_add_fusion.refs_0_, bf16[320,256]{1,0:T(8,128)(2,1)S(1)} %get-tuple-element.43.refs_2_.refs_1_, bf16[320,256]{1,0:T(8,128)(2,1)S(1)} %collective-permute-done.1.refs_2_, ...), custom_call_target="tpu_custom_call" | custom-call | flops 209715200 | tf_op jit(solution)/shard_map/direct_legendre_near/pallas_call | solution.py:41
  25.8 0.6 collective-permute-start.6
  26.4 3.0 %collective-permute-start.7 = (bf16[320,256]{1,0:T(8,128)(2,1)S(1)}, bf16[320,256]{1,0:T(8,128)(2,1)S(1)}, u32[]{:S(2)}, u32[]{:S(2)}) collective-permute-start(bf16[320,256]{1,0:T(8,128)(2,1)S(1)} %get-tuple-element.53), channel_id=1, source_target_pairs={{0,8},{4,12},{8,0},{12,4},{1,9},{5,13},{9,1},{13,5},{2,10},{6,14},... | collective-permute-start | bytes 491528 | tf_op jit(solution)/shard_map/ppermute | solution.py:244
  29.4 1.0 %spread_modes.1 = (bf16[256,256]{1,0:T(8,128)(2,1)S(1)}, bf16[256,256]{1,0:T(8,128)(2,1)S(1)}, f32[640,256]{1,0:T(8,128)S(1)}) custom-call(s32[4]{0:T(128)S(1)} %pad_add_fusion.refs_0_, bf16[128,128]{1,0:T(8,128)(2,1)S(1)} %copy-done.3, bf16[128,128]{1,0:T(8,128)(2,1)S(1)} %copy-done.4, f32[1,128]{1,0:T(1,128)S(1)} %bitcast.12, ...), custom_call_target="tpu_custom_call" | custom-call | flops 25165824 | tf_op jit(solution)/shard_map/spread_modes/pallas_call | solution.py:41
  30.4 1.6 %collective-permute-done.6.refs_1_ = bf16[320,256]{1,0:T(8,128)(2,1)S(1)} collective-permute-done((bf16[320,256]{1,0:T(8,128)(2,1)S(1)}, bf16[320,256]{1,0:T(8,128)(2,1)S(1)}, u32[]{:S(2)}, u32[]{:S(2)}) %collective-permute-start.6) | collective-permute-done | bytes 163872 | tf_op jit(solution)/shard_map/ppermute | solution.py:244
  32.0 3.9 %collective-permute-start.9 = (bf16[320,256]{1,0:T(8,128)(2,1)S(1)}, bf16[320,256]{1,0:T(8,128)(2,1)S(1)}, u32[]{:S(2)}, u32[]{:S(2)}) collective-permute-start(bf16[320,256]{1,0:T(8,128)(2,1)S(1)} %get-tuple-element.61), channel_id=1, source_target_pairs={{0,4},{4,8},{8,12},{12,0},{1,5},{5,9},{9,13},{13,1},{2,6},{6,10},{... | collective-permute-start | bytes 491528 | tf_op jit(solution)/shard_map/ppermute | solution.py:244
  36.0 1.0 %collective-permute-done.7.refs_3_ = bf16[320,256]{1,0:T(8,128)(2,1)S(1)} collective-permute-done((bf16[320,256]{1,0:T(8,128)(2,1)S(1)}, bf16[320,256]{1,0:T(8,128)(2,1)S(1)}, u32[]{:S(2)}, u32[]{:S(2)}) %collective-permute-start.7) | collective-permute-done | bytes 163872 | tf_op jit(solution)/shard_map/ppermute | solution.py:244
  37.0 3.7 %collective-permute-start.10 = (bf16[320,256]{1,0:T(8,128)(2,1)S(1)}, bf16[320,256]{1,0:T(8,128)(2,1)S(1)}, u32[]{:S(2)}, u32[]{:S(2)}) collective-permute-start(bf16[320,256]{1,0:T(8,128)(2,1)S(1)} %get-tuple-element.62), channel_id=1, source_target_pairs={{0,12},{4,0},{8,4},{12,8},{1,13},{5,1},{9,5},{13,9},{2,14},{6,2},{... | collective-permute-start | bytes 491528 | tf_op jit(solution)/shard_map/ppermute | solution.py:244
  40.6 0.4 direct_legendre_far.2.refs_0_
  41.0 0.4 vertical_solve.2
  41.5 1.7 %collective-permute-start.8 = (bf16[320,256]{1,0:T(8,128)(2,1)S(1)}, bf16[320,256]{1,0:T(8,128)(2,1)S(1)}, u32[]{:S(2)}, u32[]{:S(2)}) collective-permute-start(bf16[320,256]{1,0:T(8,128)(2,1)S(1)} %get-tuple-element.60), channel_id=1, source_target_pairs={{0,2},{2,0},{1,3},{3,1},{4,6},{6,4},{5,7},{7,5},{8,10},{10,8},{9,1... | collective-permute-start | bytes 491528 | tf_op jit(solution)/shard_map/ppermute | solution.py:244
  43.1 0.5 inverse_legendre_far.2.refs_1_
  43.7 0.5 collective-permute-done.10.refs_4_
  44.2 3.1 %collective-permute-done.8.refs_2_.refs_1_ = bf16[320,256]{1,0:T(8,128)(2,1)S(1)} collective-permute-done((bf16[320,256]{1,0:T(8,128)(2,1)S(1)}, bf16[320,256]{1,0:T(8,128)(2,1)S(1)}, u32[]{:S(2)}, u32[]{:S(2)}) %collective-permute-start.8) | collective-permute-done | bytes 163872 | tf_op jit(solution)/shard_map/ppermute | solution.py:244
  47.3 1.0 %direct_legendre_near.3 = (bf16[320,256]{1,0:T(8,128)(2,1)S(1)}, bf16[1280,256]{1,0:T(8,128)(2,1)S(1)}) custom-call(s32[4]{0:T(128)S(1)} %pad_add_fusion.refs_0_, bf16[320,256]{1,0:T(8,128)(2,1)S(1)} %get-tuple-element.55.refs_2_.refs_1_, bf16[320,256]{1,0:T(8,128)(2,1)S(1)} %collective-permute-done.9.refs_2_, ...), custom_call_target="tpu_custom_call" | custom-call | flops 209715200 | tf_op jit(solution)/shard_map/direct_legendre_near/pallas_call | solution.py:41
  48.2 1.6 %collective-permute-start.14 = (bf16[320,256]{1,0:T(8,128)(2,1)S(1)}, bf16[320,256]{1,0:T(8,128)(2,1)S(1)}, u32[]{:S(2)}, u32[]{:S(2)}) collective-permute-start(bf16[320,256]{1,0:T(8,128)(2,1)S(1)} %get-tuple-element.69), channel_id=1, source_target_pairs={{0,2},{2,0},{1,3},{3,1},{4,6},{6,4},{5,7},{7,5},{8,10},{10,8},{9,1... | collective-permute-start | bytes 491528 | tf_op jit(solution)/shard_map/ppermute | solution.py:244
  49.9 1.2 %inverse_legendre_near.2 = (bf16[320,256]{1,0:T(8,128)(2,1)S(1)}, bf16[320,256]{1,0:T(8,128)(2,1)S(1)}, bf16[320,256]{1,0:T(8,128)(2,1)S(1)}, bf16[320,256]{1,0:T(8,128)(2,1)S(1)}) custom-call(s32[4]{0:T(128)S(1)} %pad_add_fusion.refs_0_, f32[1280,256]{1,0:T(8,128)S(1)} %inverse_legendre_far.2.refs_1_, ...), custom_call_target="tpu_custom_call" | custom-call | flops 209715200 | tf_op jit(solution)/shard_map/inverse_legendre_near/pallas_call | solution.py:41
  51.1 3.5 %collective-permute-start.17 = (bf16[320,256]{1,0:T(8,128)(2,1)S(1)}, bf16[320,256]{1,0:T(8,128)(2,1)S(1)}, u32[]{:S(2)}, u32[]{:S(2)}) collective-permute-start(bf16[320,256]{1,0:T(8,128)(2,1)S(1)} %get-tuple-element.73), channel_id=1, source_target_pairs={{0,4},{4,8},{8,12},{12,0},{1,5},{5,9},{9,13},{13,1},{2,6},{6,10},{... | collective-permute-start | bytes 491528 | tf_op jit(solution)/shard_map/ppermute | solution.py:244
  54.6 2.3 %collective-permute-start.18 = (bf16[320,256]{1,0:T(8,128)(2,1)S(1)}, bf16[320,256]{1,0:T(8,128)(2,1)S(1)}, u32[]{:S(2)}, u32[]{:S(2)}) collective-permute-start(bf16[320,256]{1,0:T(8,128)(2,1)S(1)} %get-tuple-element.74), channel_id=1, source_target_pairs={{0,12},{4,0},{8,4},{12,8},{1,13},{5,1},{9,5},{13,9},{2,14},{6,2},{... | collective-permute-start | bytes 491528 | tf_op jit(solution)/shard_map/ppermute | solution.py:244
  56.9 5.9 %collective-permute-done.15.refs_3_ = bf16[320,256]{1,0:T(8,128)(2,1)S(1)} collective-permute-done((bf16[320,256]{1,0:T(8,128)(2,1)S(1)}, bf16[320,256]{1,0:T(8,128)(2,1)S(1)}, u32[]{:S(2)}, u32[]{:S(2)}) %collective-permute-start.15) | collective-permute-done | bytes 163872 | tf_op jit(solution)/shard_map/ppermute | solution.py:244
  62.8 0.4 direct_legendre_far.3.refs_0_
  63.2 0.4 vertical_solve.3
  63.7 0.7 collective-permute-start.16
  64.3 0.5 inverse_legendre_far.3.refs_1_
  64.9 4.1 %collective-permute-done.16.refs_2_.refs_3_ = bf16[320,256]{1,0:T(8,128)(2,1)S(1)} collective-permute-done((bf16[320,256]{1,0:T(8,128)(2,1)S(1)}, bf16[320,256]{1,0:T(8,128)(2,1)S(1)}, u32[]{:S(2)}, u32[]{:S(2)}) %collective-permute-start.16) | collective-permute-done | bytes 163872 | tf_op jit(solution)/shard_map/ppermute | solution.py:244
  69.0 1.2 %inverse_legendre_near.3 = (bf16[320,256]{1,0:T(8,128)(2,1)S(1)}, bf16[320,256]{1,0:T(8,128)(2,1)S(1)}, bf16[320,256]{1,0:T(8,128)(2,1)S(1)}, bf16[320,256]{1,0:T(8,128)(2,1)S(1)}) custom-call(s32[4]{0:T(128)S(1)} %pad_add_fusion.refs_0_, f32[1280,256]{1,0:T(8,128)S(1)} %inverse_legendre_far.3.refs_1_, ...), custom_call_target="tpu_custom_call" | custom-call | flops 209715200 | tf_op jit(solution)/shard_map/inverse_legendre_near/pallas_call | solution.py:41
  70.2 0.7 collective-permute-start.19
  71.0 3.4 %collective-permute-start.20 = (bf16[320,256]{1,0:T(8,128)(2,1)S(1)}, bf16[320,256]{1,0:T(8,128)(2,1)S(1)}, u32[]{:S(2)}, u32[]{:S(2)}) collective-permute-start(bf16[320,256]{1,0:T(8,128)(2,1)S(1)} %get-tuple-element.82), channel_id=1, source_target_pairs={{0,8},{4,12},{8,0},{12,4},{1,9},{5,13},{9,1},{13,5},{2,10},{6,14},... | collective-permute-start | bytes 491528 | tf_op jit(solution)/shard_map/ppermute | solution.py:244
  74.3 1.7 %order_spectral.1 = bf16[2560,128]{1,0:T(8,128)(2,1)} custom-call(s32[4]{0:T(128)S(1)} %pad_add_fusion.refs_0_, bf16[320,256]{1,0:T(8,128)(2,1)S(1)} %collective-permute-done.8.refs_2_.refs_1_, bf16[320,256]{1,0:T(8,128)(2,1)S(1)} %get-tuple-element.59.refs_0_.refs_2_, bf16[320,256]{1,0:T(8,128)(2,1)S(1)} %collective-permute-done.16.refs_2_.refs_3_, ...), custom_call_target="tpu_custom_call" | custom-call | tf_op jit(solution)/shard_map/order_spectral/pallas_call | solution.py:41
  76.1 2.7 %collective-permute-done.19.refs_6_ = bf16[320,256]{1,0:T(8,128)(2,1)S(1)} collective-permute-done((bf16[320,256]{1,0:T(8,128)(2,1)S(1)}, bf16[320,256]{1,0:T(8,128)(2,1)S(1)}, u32[]{:S(2)}, u32[]{:S(2)}) %collective-permute-start.19) | collective-permute-done | bytes 163872 | tf_op jit(solution)/shard_map/ppermute | solution.py:244
  78.8 4.1 %collective-permute-done.20.refs_7_ = bf16[320,256]{1,0:T(8,128)(2,1)S(1)} collective-permute-done((bf16[320,256]{1,0:T(8,128)(2,1)S(1)}, bf16[320,256]{1,0:T(8,128)(2,1)S(1)}, u32[]{:S(2)}, u32[]{:S(2)}) %collective-permute-start.20) | collective-permute-done | bytes 163872 | tf_op jit(solution)/shard_map/ppermute | solution.py:244
  82.9 2.2 %join_hemispheres.1 = bf16[2,2560,128]{2,1,0:T(8,128)(2,1)} custom-call(s32[4]{0:T(128)S(1)} %pad_add_fusion.refs_0_, bf16[320,256]{1,0:T(8,128)(2,1)S(1)} %get-tuple-element.64.refs_1_, bf16[320,256]{1,0:T(8,128)(2,1)S(1)} %collective-permute-done.17.refs_2_, bf16[320,256]{1,0:T(8,128)(2,1)S(1)} %collective-permute-done.15.refs_3_, ...), custom_call_target="tpu_custom_call" | custom-call | flops 335544320 | tf_op jit(solution)/shard_map/join_hemispheres/pallas_call | solution.py:41
  (28 shorter events, 0.3 us)
Async XLA Ops:
  1.5 1.3 %copy-start = (bf16[2,320,4,2,128]{4,3,2,1,0:T(2,128)(2,1)S(1)}, bf16[2,320,4,2,128]{4,3,2,1,0:T(2,128)(2,1)}, u32[]{:S(2)}) copy-start(bf16[2,320,4,2,128]{4,3,2,1,0:T(2,128)(2,1)} %param.6) | copy-start | bytes 3932164
  2.8 11.7 %copy-start.1 = (bf16[2,320,4,2,128]{4,3,2,1,0:T(2,128)(2,1)S(1)}, bf16[2,320,4,2,128]{4,3,2,1,0:T(2,128)(2,1)}, u32[]{:S(2)}) copy-start(bf16[2,320,4,2,128]{4,3,2,1,0:T(2,128)(2,1)} %param.6) | copy-start | bytes 3932164
  3.9 1.1 %copy-start.2 = (bf16[1,320,1280]{2,1,0:T(8,128)(2,1)S(1)}, bf16[1,320,1280]{2,1,0:T(8,128)(2,1)}, u32[]{:S(2)}) copy-start(bf16[1,320,1280]{2,1,0:T(8,128)(2,1)} %param.7) | copy-start | bytes 2457604
  6.0 8.6 %collective-permute-start.4 = (bf16[160,1280]{1,0:T(8,128)(2,1)S(1)}, bf16[160,1280]{1,0:T(8,128)(2,1)S(1)}, u32[]{:S(2)}, u32[]{:S(2)}) collective-permute-start(bf16[160,1280]{1,0:T(8,128)(2,1)S(1)} %split_table.2.refs_5_.refs_3_), channel_id=1, source_target_pairs={{0,1},{1,0},{2,3},{3,2},{4,5},{5,4},{6,7},{7,6},{8,9},{9,8},{10,11... | collective-permute-start | bytes 1228808 | tf_op jit(solution)/shard_map/ppermute | solution.py:244
  6.5 17.8 %collective-permute-start = (bf16[160,1280]{1,0:T(8,128)(2,1)S(1)}, bf16[160,1280]{1,0:T(8,128)(2,1)S(1)}, u32[]{:S(2)}, u32[]{:S(2)}) collective-permute-start(bf16[160,1280]{1,0:T(8,128)(2,1)S(1)} %split_table.2.refs_5_.refs_3_), channel_id=1, source_target_pairs={{0,2},{2,0},{1,3},{3,1},{4,6},{6,4},{5,7},{7,5},{8,10},{10,8},{9,1... | collective-permute-start | bytes 1228808 | tf_op jit(solution)/shard_map/ppermute | solution.py:244
  9.1 8.9 %collective-permute-start.1 = (bf16[320,256]{1,0:T(8,128)(2,1)S(1)}, bf16[320,256]{1,0:T(8,128)(2,1)S(1)}, u32[]{:S(2)}, u32[]{:S(2)}) collective-permute-start(bf16[320,256]{1,0:T(8,128)(2,1)S(1)} %get-tuple-element.44), channel_id=1, source_target_pairs={{0,4},{4,8},{8,12},{12,0},{1,5},{5,9},{9,13},{13,1},{2,6},{6,10},{... | collective-permute-start | bytes 491528 | tf_op jit(solution)/shard_map/ppermute | solution.py:244
  10.6 13.7 %collective-permute-start.2 = (bf16[320,256]{1,0:T(8,128)(2,1)S(1)}, bf16[320,256]{1,0:T(8,128)(2,1)S(1)}, u32[]{:S(2)}, u32[]{:S(2)}) collective-permute-start(bf16[320,256]{1,0:T(8,128)(2,1)S(1)} %get-tuple-element.45), channel_id=1, source_target_pairs={{0,8},{4,12},{8,0},{12,4},{1,9},{5,13},{9,1},{13,5},{2,10},{6,14},... | collective-permute-start | bytes 491528 | tf_op jit(solution)/shard_map/ppermute | solution.py:244
  13.2 11.1 %collective-permute-start.3 = (bf16[320,256]{1,0:T(8,128)(2,1)S(1)}, bf16[320,256]{1,0:T(8,128)(2,1)S(1)}, u32[]{:S(2)}, u32[]{:S(2)}) collective-permute-start(bf16[320,256]{1,0:T(8,128)(2,1)S(1)} %get-tuple-element.46), channel_id=1, source_target_pairs={{0,12},{4,0},{8,4},{12,8},{1,13},{5,1},{9,5},{13,9},{2,14},{6,2},{... | collective-permute-start | bytes 491528 | tf_op jit(solution)/shard_map/ppermute | solution.py:244
  15.6 13.7 %copy-start.3 = (bf16[128,128]{1,0:T(8,128)(2,1)S(1)}, bf16[128,128]{1,0:T(8,128)(2,1)}, u32[]{:S(2)}) copy-start(bf16[128,128]{1,0:T(8,128)(2,1)} %refs_1_.1) | copy-start | bytes 98308
  15.7 13.7 %copy-start.4 = (bf16[128,128]{1,0:T(8,128)(2,1)S(1)}, bf16[128,128]{1,0:T(8,128)(2,1)}, u32[]{:S(2)}) copy-start(bf16[128,128]{1,0:T(8,128)(2,1)} %refs_2_.1) | copy-start | bytes 98308
  15.7 13.7 %copy-start.5 = (f32[128]{0:T(128)S(1)}, f32[128]{0:T(128)}, u32[]{:S(2)}) copy-start(f32[128]{0:T(128)} %param.11) | copy-start | bytes 1540
  16.6 12.8 %collective-permute-start.12 = (bf16[160,1280]{1,0:T(8,128)(2,1)S(1)}, bf16[160,1280]{1,0:T(8,128)(2,1)S(1)}, u32[]{:S(2)}, u32[]{:S(2)}) collective-permute-start(bf16[160,1280]{1,0:T(8,128)(2,1)S(1)} %split_table.3.refs_4_.refs_5_.refs_3_), channel_id=1, source_target_pairs={{0,2},{2,0},{1,3},{3,1},{4,6},{6,4},{5,7},{7,5},{8,10},{10,8},{9,1... | collective-permute-start | bytes 1228808 | tf_op jit(solution)/shard_map/ppermute | solution.py:244
  24.3 16.3 %collective-permute-start.5 = (bf16[160,1280]{1,0:T(8,128)(2,1)S(1)}, bf16[160,1280]{1,0:T(8,128)(2,1)S(1)}, u32[]{:S(2)}, u32[]{:S(2)}) collective-permute-start(bf16[160,1280]{1,0:T(8,128)(2,1)S(1)} %collective-permute-done.refs_1_), channel_id=1, source_target_pairs={{0,1},{1,0},{2,3},{3,2},{4,5},{5,4},{6,7},{7,6},{8,9},{9,8},{10,11... | collective-permute-start | bytes 1228808 | tf_op jit(solution)/shard_map/ppermute | solution.py:244
  24.3 23.0 %collective-permute-start.11 = (bf16[160,1280]{1,0:T(8,128)(2,1)S(1)}, bf16[160,1280]{1,0:T(8,128)(2,1)S(1)}, u32[]{:S(2)}, u32[]{:S(2)}) collective-permute-start(bf16[160,1280]{1,0:T(8,128)(2,1)S(1)} %split_table.3.refs_4_.refs_5_.refs_3_), channel_id=1, source_target_pairs={{0,1},{1,0},{2,3},{3,2},{4,5},{5,4},{6,7},{7,6},{8,9},{9,8},{10,11... | collective-permute-start | bytes 1228808 | tf_op jit(solution)/shard_map/ppermute | solution.py:244
  25.8 6.2 %collective-permute-start.6 = (bf16[320,256]{1,0:T(8,128)(2,1)S(1)}, bf16[320,256]{1,0:T(8,128)(2,1)S(1)}, u32[]{:S(2)}, u32[]{:S(2)}) collective-permute-start(bf16[320,256]{1,0:T(8,128)(2,1)S(1)} %get-tuple-element.52), channel_id=1, source_target_pairs={{0,2},{2,0},{1,3},{3,1},{4,6},{6,4},{5,7},{7,5},{8,10},{10,8},{9,1... | collective-permute-start | bytes 491528 | tf_op jit(solution)/shard_map/ppermute | solution.py:244
  26.4 10.6 %collective-permute-start.7 = (bf16[320,256]{1,0:T(8,128)(2,1)S(1)}, bf16[320,256]{1,0:T(8,128)(2,1)S(1)}, u32[]{:S(2)}, u32[]{:S(2)}) collective-permute-start(bf16[320,256]{1,0:T(8,128)(2,1)S(1)} %get-tuple-element.53), channel_id=1, source_target_pairs={{0,8},{4,12},{8,0},{12,4},{1,9},{5,13},{9,1},{13,5},{2,10},{6,14},... | collective-permute-start | bytes 491528 | tf_op jit(solution)/shard_map/ppermute | solution.py:244
  29.4 33.5 %collective-permute-start.13 = (bf16[160,1280]{1,0:T(8,128)(2,1)S(1)}, bf16[160,1280]{1,0:T(8,128)(2,1)S(1)}, u32[]{:S(2)}, u32[]{:S(2)}) collective-permute-start(bf16[160,1280]{1,0:T(8,128)(2,1)S(1)} %collective-permute-done.12.refs_1_), channel_id=1, source_target_pairs={{0,1},{1,0},{2,3},{3,2},{4,5},{5,4},{6,7},{7,6},{8,9},{9,8},{10,11... | collective-permute-start | bytes 1228808 | tf_op jit(solution)/shard_map/ppermute | solution.py:244
  32.0 11.7 %collective-permute-start.9 = (bf16[320,256]{1,0:T(8,128)(2,1)S(1)}, bf16[320,256]{1,0:T(8,128)(2,1)S(1)}, u32[]{:S(2)}, u32[]{:S(2)}) collective-permute-start(bf16[320,256]{1,0:T(8,128)(2,1)S(1)} %get-tuple-element.61), channel_id=1, source_target_pairs={{0,4},{4,8},{8,12},{12,0},{1,5},{5,9},{9,13},{13,1},{2,6},{6,10},{... | collective-permute-start | bytes 491528 | tf_op jit(solution)/shard_map/ppermute | solution.py:244
  37.0 7.2 %collective-permute-start.10 = (bf16[320,256]{1,0:T(8,128)(2,1)S(1)}, bf16[320,256]{1,0:T(8,128)(2,1)S(1)}, u32[]{:S(2)}, u32[]{:S(2)}) collective-permute-start(bf16[320,256]{1,0:T(8,128)(2,1)S(1)} %get-tuple-element.62), channel_id=1, source_target_pairs={{0,12},{4,0},{8,4},{12,8},{1,13},{5,1},{9,5},{13,9},{2,14},{6,2},{... | collective-permute-start | bytes 491528 | tf_op jit(solution)/shard_map/ppermute | solution.py:244
  41.5 5.8 %collective-permute-start.8 = (bf16[320,256]{1,0:T(8,128)(2,1)S(1)}, bf16[320,256]{1,0:T(8,128)(2,1)S(1)}, u32[]{:S(2)}, u32[]{:S(2)}) collective-permute-start(bf16[320,256]{1,0:T(8,128)(2,1)S(1)} %get-tuple-element.60), channel_id=1, source_target_pairs={{0,2},{2,0},{1,3},{3,1},{4,6},{6,4},{5,7},{7,5},{8,10},{10,8},{9,1... | collective-permute-start | bytes 491528 | tf_op jit(solution)/shard_map/ppermute | solution.py:244
  48.2 8.6 %collective-permute-start.14 = (bf16[320,256]{1,0:T(8,128)(2,1)S(1)}, bf16[320,256]{1,0:T(8,128)(2,1)S(1)}, u32[]{:S(2)}, u32[]{:S(2)}) collective-permute-start(bf16[320,256]{1,0:T(8,128)(2,1)S(1)} %get-tuple-element.69), channel_id=1, source_target_pairs={{0,2},{2,0},{1,3},{3,1},{4,6},{6,4},{5,7},{7,5},{8,10},{10,8},{9,1... | collective-permute-start | bytes 491528 | tf_op jit(solution)/shard_map/ppermute | solution.py:244
  51.0 11.8 %collective-permute-start.15 = (bf16[320,256]{1,0:T(8,128)(2,1)S(1)}, bf16[320,256]{1,0:T(8,128)(2,1)S(1)}, u32[]{:S(2)}, u32[]{:S(2)}) collective-permute-start(bf16[320,256]{1,0:T(8,128)(2,1)S(1)} %get-tuple-element.70), channel_id=1, source_target_pairs={{0,8},{4,12},{8,0},{12,4},{1,9},{5,13},{9,1},{13,5},{2,10},{6,14},... | collective-permute-start | bytes 491528 | tf_op jit(solution)/shard_map/ppermute | solution.py:244
  51.1 13.8 %collective-permute-start.17 = (bf16[320,256]{1,0:T(8,128)(2,1)S(1)}, bf16[320,256]{1,0:T(8,128)(2,1)S(1)}, u32[]{:S(2)}, u32[]{:S(2)}) collective-permute-start(bf16[320,256]{1,0:T(8,128)(2,1)S(1)} %get-tuple-element.73), channel_id=1, source_target_pairs={{0,4},{4,8},{8,12},{12,0},{1,5},{5,9},{9,13},{13,1},{2,6},{6,10},{... | collective-permute-start | bytes 491528 | tf_op jit(solution)/shard_map/ppermute | solution.py:244
  54.6 10.3 %collective-permute-start.18 = (bf16[320,256]{1,0:T(8,128)(2,1)S(1)}, bf16[320,256]{1,0:T(8,128)(2,1)S(1)}, u32[]{:S(2)}, u32[]{:S(2)}) collective-permute-start(bf16[320,256]{1,0:T(8,128)(2,1)S(1)} %get-tuple-element.74), channel_id=1, source_target_pairs={{0,12},{4,0},{8,4},{12,8},{1,13},{5,1},{9,5},{13,9},{2,14},{6,2},{... | collective-permute-start | bytes 491528 | tf_op jit(solution)/shard_map/ppermute | solution.py:244
  63.7 5.4 %collective-permute-start.16 = (bf16[320,256]{1,0:T(8,128)(2,1)S(1)}, bf16[320,256]{1,0:T(8,128)(2,1)S(1)}, u32[]{:S(2)}, u32[]{:S(2)}) collective-permute-start(bf16[320,256]{1,0:T(8,128)(2,1)S(1)} %get-tuple-element.72), channel_id=1, source_target_pairs={{0,2},{2,0},{1,3},{3,1},{4,6},{6,4},{5,7},{7,5},{8,10},{10,8},{9,1... | collective-permute-start | bytes 491528 | tf_op jit(solution)/shard_map/ppermute | solution.py:244
  70.2 8.6 %collective-permute-start.19 = (bf16[320,256]{1,0:T(8,128)(2,1)S(1)}, bf16[320,256]{1,0:T(8,128)(2,1)S(1)}, u32[]{:S(2)}, u32[]{:S(2)}) collective-permute-start(bf16[320,256]{1,0:T(8,128)(2,1)S(1)} %get-tuple-element.81), channel_id=1, source_target_pairs={{0,4},{4,8},{8,12},{12,0},{1,5},{5,9},{9,13},{13,1},{2,6},{6,10},{... | collective-permute-start | bytes 491528 | tf_op jit(solution)/shard_map/ppermute | solution.py:244
  71.0 11.9 %collective-permute-start.20 = (bf16[320,256]{1,0:T(8,128)(2,1)S(1)}, bf16[320,256]{1,0:T(8,128)(2,1)S(1)}, u32[]{:S(2)}, u32[]{:S(2)}) collective-permute-start(bf16[320,256]{1,0:T(8,128)(2,1)S(1)} %get-tuple-element.82), channel_id=1, source_target_pairs={{0,8},{4,12},{8,0},{12,4},{1,9},{5,13},{9,1},{13,5},{2,10},{6,14},... | collective-permute-start | bytes 491528 | tf_op jit(solution)/shard_map/ppermute | solution.py:244
  74.3 8.5 %collective-permute-start.21 = (bf16[320,256]{1,0:T(8,128)(2,1)S(1)}, bf16[320,256]{1,0:T(8,128)(2,1)S(1)}, u32[]{:S(2)}, u32[]{:S(2)}) collective-permute-start(bf16[320,256]{1,0:T(8,128)(2,1)S(1)} %get-tuple-element.83), channel_id=1, source_target_pairs={{0,12},{4,0},{8,4},{12,8},{1,13},{5,1},{9,5},{13,9},{2,14},{6,2},{... | collective-permute-start | bytes 491528 | tf_op jit(solution)/shard_map/ppermute | solution.py:244

commit v2 on v1

--- a/solution.py
+++ b/solution.py
@@ -54,7 +54,7 @@
     return run
 
 
-def split_body(slots, fields, block, odd, meta_ref, rows_ref, weight_ref, *outs):
+def split_body(slots, fields, block, meta_ref, rows_ref, weight_ref, *outs):
     latitudes = weight_ref.shape[0]
     group = slots * fields
     size = block * group
@@ -67,24 +67,29 @@
         south = rows_ref[1, first * group : first * group + size, :]
         sorted_rows = dot32(order, jnp.concatenate((north, south), axis=1))
         up, down = sorted_rows[:, :128], sorted_rows[:, 128:]
-        mixed = up - down if odd else up + down
         weight = weight_ref[first : first + block, :]
-        for shift in range(slots):
-            for field in range(fields):
-                at = (shift * fields + field) * block
-                outs[shift][first : first + block, field * 128 : field * 128 + 128] = (
-                    weight * mixed[at : at + block]
-                ).astype(jnp.bfloat16)
-
-
-def table_body(odd, meta_ref, table_ref, out_ref):
-    rows, columns = table_ref.shape
+        for odd, mixed in enumerate((up + down, up - down)):
+            for shift in range(slots):
+                for field in range(fields):
+                    at = (shift * fields + field) * block
+                    outs[odd * slots + shift][first : first + block, field * 128 : field * 128 + 128] = (
+                        weight * mixed[at : at + block]
+                    ).astype(jnp.bfloat16)
+
+
+def table_body(meta_ref, first_ref, second_ref, even_ref, odd_ref):
+    rows, columns = first_ref.shape
     half = rows // 2
-    out_row, in_row = iota2((half, rows), 0), iota2((half, rows), 1)
-    order = picks(in_row == 2 * out_row + (meta_ref[0] + odd) % 2)
-    for first in range(0, columns, 256):
-        lanes = slice(first, first + 256)
-        out_ref[:, lanes] = dot32(order, table_ref[:, lanes]).astype(jnp.bfloat16)
+    out_row, in_row = iota2((rows, rows), 0), iota2((rows, rows), 1)
+    odd = jnp.where(out_row < half, 0, 1)
+    order = picks(in_row == 2 * (out_row - odd * half) + (meta_ref[0] + odd) % 2)
+    for g, table_ref in enumerate((first_ref, second_ref)):
+        at = slice(g * half, g * half + half)
+        for first in range(0, columns, 256):
+            lanes = slice(first, first + 256)
+            result = dot32(order, table_ref[:, lanes]).astype(jnp.bfloat16)
+            even_ref[at, lanes] = result[:half]
+            odd_ref[at, lanes] = result[half:]
 
 
 def modes_body(flds, degree_total, meta_ref, to_ref, from_ref, rate_ref, in_ref, out_ref, scale_ref):
@@ -119,18 +124,16 @@
 
 
 def near_body(meta_ref, *refs):
-    parts, tables, (out_ref, data_ref) = refs[:-4], refs[-4:-2], refs[-2:]
+    parts, (table_ref, out_ref, data_ref) = refs[:-3], refs[-3:]
     wide, latitudes = len(parts), parts[0].shape[0]
     for shift in range(wide):
         owner = lax.rem(meta_ref[1] - shift + wide, wide)
         data_ref[pl.ds(pl.multiple_of(owner * latitudes, latitudes), latitudes), :] = parts[shift][...]
-    table = jnp.concatenate([ref[...] for ref in tables], axis=0)
-    out_ref[...] = dot32(table, data_ref[...]).astype(jnp.bfloat16)
-
-
-def far_body(data_ref, first_ref, second_ref, out_ref):
-    table = jnp.concatenate((first_ref[...], second_ref[...]), axis=0)
-    out_ref[...] = dot32(table, data_ref[...]).astype(jnp.bfloat16)
+    out_ref[...] = dot32(table_ref[...], data_ref[...]).astype(jnp.bfloat16)
+
+
+def far_body(data_ref, table_ref, out_ref):
+    out_ref[...] = dot32(table_ref[...], data_ref[...]).astype(jnp.bfloat16)
 
 
 def solve_body(odd, own_ref, other_ref, in_ref, out_ref, scale_ref, to_own_ref, to_other_ref):
@@ -144,24 +147,24 @@
         to_other_ref[:, lanes] = result[:, 128:]
 
 
-def turned_dot(tables, spectral, chunk):
-    table = jnp.concatenate([ref[:, chunk] for ref in tables], axis=0)
-    return lax.dot_general(table, spectral, (((0,), (0,)), ((), ())), preferred_element_type=jnp.float32)
-
-
-def inverse_far_body(spectral_ref, first_ref, second_ref, out_ref):
+def turned_dot(table_ref, spectral_ref, chunk):
+    return lax.dot_general(
+        table_ref[:, chunk], spectral_ref[...], (((0,), (0,)), ((), ())), preferred_element_type=jnp.float32
+    )
+
+
+def inverse_far_body(spectral_ref, table_ref, out_ref):
     for first in range(0, out_ref.shape[0], 256):
         chunk = slice(first, first + 256)
-        out_ref[chunk, :] = turned_dot((first_ref, second_ref), spectral_ref[...], chunk)
-
-
-def inverse_near_body(meta_ref, sum_ref, spectral_ref, first_ref, second_ref, *refs):
+        out_ref[chunk, :] = turned_dot(table_ref, spectral_ref, chunk)
+
+
+def inverse_near_body(meta_ref, sum_ref, spectral_ref, table_ref, *refs):
     outs, total = refs[:-1], refs[-1]
     wide, latitudes = len(outs), outs[0].shape[0]
     for first in range(0, total.shape[0], 256):
         chunk = slice(first, first + 256)
-        more = turned_dot((first_ref, second_ref), spectral_ref[...], chunk)
-        total[chunk, :] = (sum_ref[chunk, :] + more).astype(jnp.bfloat16)
+        total[chunk, :] = (sum_ref[chunk, :] + turned_dot(table_ref, spectral_ref, chunk)).astype(jnp.bfloat16)
     for shift in range(wide):
         owner = lax.rem(meta_ref[1] + shift, wide)
         outs[shift][...] = total[pl.ds(pl.multiple_of(owner * latitudes, latitudes), latitudes), :]
@@ -257,25 +260,14 @@
     move_flops = 4 * group * latitudes * 128 * 256
     share_flops = 2 * share * half_count * columns
 
-    def split(odd, after=()):
+    def direct_near(received, table, after=()):
         return call(
-            functools.partial(split_body, slots, fields, block, odd), (shape(latitudes, columns),) * wide,
-            "split_hemispheres", move_flops, after=after,
-        )(meta, fourier_input_rows.reshape(2, latitudes * group, lanes), weights)
-
-    def split_table(odd, after):
-        return call(
-            functools.partial(table_body, odd), shape(half_rows, half_count), "split_table",
-            shard_rows * shard_rows * half_count, after=after,
-        )(meta, legendre[0])
-
-    def direct_near(received, table):
-        return call(
-            near_body, (shape(share, columns), shape(half_count, columns)), "direct_legendre_near", share_flops
-        )(meta, *received, *table)
+            near_body, (shape(share, columns), shape(half_count, columns)), "direct_legendre_near", share_flops,
+            after=after,
+        )(meta, *received, table)
 
     def direct_far(data, table):
-        return call(far_body, shape(share, columns), "direct_legendre_far", share_flops, scalars=0)(data, *table)
+        return call(far_body, shape(share, columns), "direct_legendre_far", share_flops, scalars=0)(data, table)
 
     def solve(odd, own, other):
         return call(
@@ -286,13 +278,13 @@
     def inverse_far(spectral, table):
         return call(
             inverse_far_body, shape(half_count, columns, kind=f32), "inverse_legendre_far", share_flops, scalars=0,
-        )(spectral, *table)
+        )(spectral, table)
 
     def inverse_near(total, spectral, table):
         return call(
             inverse_near_body, (shape(latitudes, columns),) * wide, "inverse_legendre_near", share_flops,
             scratch=[pltpu.VMEM((half_count, columns), bf16)],
-        )(meta, total, spectral, *table)
+        )(meta, total, spectral, table)
 
     def over_lev(value):
         return shifted(value, "lev", levs, 1)
@@ -300,38 +292,46 @@
     def beside(value):
         return shifted(value, "fld", flds, 1)
 
-    even = split(0)
-    even_in = [even[0]] + [across(even[step], step) for step in range(1, wide)]
-    part = split_table(0, (even[0],))
-    even_near, even_far = [part, beside(part)], over_lev(part)
-    even_far, *even_in[1:] = behind(even_far, *even_in[1:])
-    even_far = [even_far, beside(even_far)]
-    odd = split(1, (even_near[1],))
-    odd_part = split_table(1, (odd[0],))
+    blocks = call(
+        functools.partial(split_body, slots, fields, block), (shape(latitudes, columns),) * (2 * wide),
+        "split_hemispheres", move_flops,
+    )(meta, fourier_input_rows.reshape(2, latitudes * group, lanes), weights)
+    table_beside, *blocks = behind(beside(legendre[0]), *blocks)
+    even_in, odd_in = (
+        [half[0]] + [across(half[step], step) for step in range(1, wide)] for half in (blocks[:wide], blocks[wide:])
+    )
+    def split_table(first, second, after=()):
+        return call(
+            table_body, (shape(flds * half_rows, half_count),) * 2, "split_table",
+            4 * shard_rows * shard_rows * half_count, after=after,
+        )(meta, first, second)
+
+    far_part = over_lev(legendre[0])
+    even_near, odd_near = split_table(legendre[0], table_beside)
     *matrices, scale = call(
         functools.partial(modes_body, flds, degree_count),
         (shape(2 * levels, 2 * levels),) * 2 + (shape(2 * share, 2 * levels, kind=f32),),
-        "spread_modes", 12 * levels * levels * levels, after=(odd_part,),
+        "spread_modes", 12 * levels * levels * levels, after=(blocks[0],),
     )(meta, to_modes, from_modes, mode_rate[None, :])
     matrices = (*matrices, scale)
 
-    odd_in = [odd[0]] + [across(odd[step], step) for step in range(1, wide)]
-    odd_near, odd_far = [odd_part, beside(odd_part)], over_lev(odd_part)
-    odd_far = [odd_far, beside(odd_far)]
-    raw, data = direct_near(even_in, even_near)
+    even_in[1], odd_in[1] = behind(even_in[1], odd_in[1])
+    raw, data = direct_near(even_in, even_near, (scale,))
+    far_part, raw = behind(far_part, raw)
+    even_far, odd_far = split_table(far_part, beside(far_part))
     other, odd_in[2] = behind(over_lev(raw), odd_in[2])
     to_own, to_other = solve(0, direct_far(data, even_far), other)
     total = inverse_far(to_own, even_far)
-    from_other, odd_in[1], odd_in[3] = behind(over_lev(to_other), odd_in[1], odd_in[3])
+    from_other = over_lev(to_other)
     even_spectral = [from_other, to_own]
     grid = inverse_near(total, from_other, even_near)
 
     even_out = [grid[0]] + [across(grid[step], step) for step in range(1, wide)]
-    raw, data = direct_near(odd_in, odd_near)
-    other, even_out[2] = behind(over_lev(raw), even_out[2])
+    raw, data = direct_near(odd_in, odd_near, (grid[0],))
+    other, even_out[1] = behind(over_lev(raw), even_out[1])
     to_own, to_other = solve(1, direct_far(data, odd_far), other)
     total = inverse_far(to_own, odd_far)
-    from_other, even_out[1], even_out[3] = behind(over_lev(to_other), even_out[1], even_out[3])
+    from_other, even_out[2], even_out[3] = behind(over_lev(to_other), even_out[2], even_out[3])
     odd_spectral = [from_other, to_own]
     grid = inverse_near(total, from_other, odd_near)
     odd_out = [grid[0]] + [across(grid[step], step) for step in range(1, wide)]

time: 85.2 us -> 85 us (level); the launches traced: 85 us -> 83.7 us
  starting transfers between devices: 34.7 us -> 33.4 us
  local copies, waits for them, and re-layouts: 2.58 us -> 1.44 us
  waiting for transfers between devices: 30.2 us -> 31.2 us
    ppermute x22 -> x19, starting transfers between devices: 34.7 us -> 33.4 us  [shifted(): lax.ppermute(value, axis, [(i, (i + step) % count) for i in range(count)])]
    unnamed x12 -> x10, local copies, waits for them, and re-layouts: 2.48 us -> 1.33 us
    ppermute x22 -> x19, waiting for transfers between devices: 30.2 us -> 31.2 us  [shifted(): lax.ppermute(value, axis, [(i, (i + step) % count) for i in range(count)])]
    pallas_call x17 -> x16, Pallas kernels: 15.9 us -> 16.1 us  [run(): pl.pallas_call(kernel, out_shape=out_shape, in_specs=[smem] * scalars + [...]
  transfers between devices with their start and end apart: 22 -> 19, of which waited for: 10 -> 9; matrix products, arithmetic and copies ran while one was open for 0% -> 0% of each run, Pallas kernels for 12% -> 11%
where the time goes in v2:
time: 85 us; the launch traced here: 83.7 us
  starting transfers between devices  33.4 us (39%)
  waiting for transfers between devices  31.2 us (37%)
  Pallas kernels  16.1 us (19%)
  between operations  1.49 us (2%)
  local copies, waits for them, and re-layouts  1.44 us (2%)
    ppermute x19, starting transfers between devices, shifted(): lax.ppermute(value, axis, [(i, (i + step) % count) for i in range(count)])  33.4 us
    ppermute x19, waiting for transfers between devices, shifted(): lax.ppermute(value, axis, [(i, (i + step) % count) for i in range(count)])  31.2 us
    pallas_call x16, Pallas kernels, run(): pl.pallas_call(kernel, out_shape=out_shape, in_specs=[smem] * scalars + [...  16.1 us
  transfers between devices with their start and end apart: 19, of which 9 were waited for; matrix products, arithmetic and copies ran while one was open for 0% of the time, Pallas kernels for 11%

profile of v2, /device:TPU:0, one launch (start us, length us, event | category | flops | bytes accessed | tf_op | source)
XLA Modules:
  0.0 83.7 jit_solution(4083992583359298571)
XLA Ops:
  0.7 0.5 collective-permute-start
  1.2 2.6 %collective-permute-start.5 = (bf16[320,1280]{1,0:T(8,128)(2,1)}, bf16[320,1280]{1,0:T(8,128)(2,1)S(1)}, u32[]{:S(2)}, u32[]{:S(2)}) collective-permute-start(bf16[320,1280]{1,0:T(8,128)(2,1)} %bitcast.11), channel_id=1, source_target_pairs={{0,2},{2,0},{1,3},{3,1},{4,6},{6,4},{5,7},{7,5},{8,10},{10,8},{9,1... | collective-permute-start | bytes 2457608 | tf_op jit(solution)/shard_map/ppermute | solution.py:247
  4.4 0.1 pad_add_fusion.refs_0_
  4.5 0.1 broadcast_in_dim.4.refs_2_
  4.6 0.0 copy-start
  4.6 1.3 %copy-done = bf16[2,320,4,2,128]{4,3,2,1,0:T(2,128)(2,1)S(1)} copy-done((bf16[2,320,4,2,128]{4,3,2,1,0:T(2,128)(2,1)S(1)}, bf16[2,320,4,2,128]{4,3,2,1,0:T(2,128)(2,1)}, u32[]{:S(2)}) %copy-start) | copy-done | bytes 1310744
  6.0 1.1 %split_hemispheres.1 = (bf16[320,256]{1,0:T(8,128)(2,1)S(1)}, bf16[320,256]{1,0:T(8,128)(2,1)S(1)}, bf16[320,256]{1,0:T(8,128)(2,1)S(1)}, bf16[320,256]{1,0:T(8,...) custom-call(s32[4]{0:T(128)S(1)} %pad_add_fusion.refs_0_, ...), custom_call_target="tpu_custom_call" | custom-call | flops 335544320 | tf_op jit(solution)/shard_map/split_hemispheres/pallas_call | solution.py:41
  7.0 1.6 %collective-permute-start.1 = (bf16[320,256]{1,0:T(8,128)(2,1)S(1)}, bf16[320,256]{1,0:T(8,128)(2,1)S(1)}, u32[]{:S(2)}, u32[]{:S(2)}) collective-permute-start(bf16[320,256]{1,0:T(8,128)(2,1)S(1)} %get-tuple-element.62), channel_id=1, source_target_pairs={{0,4},{4,8},{8,12},{12,0},{1,5},{5,9},{9,13},{13,1},{2,6},{6,10},{... | collective-permute-start | bytes 491528 | tf_op jit(solution)/shard_map/ppermute | solution.py:247
  8.7 1.6 %collective-permute-start.2 = (bf16[320,256]{1,0:T(8,128)(2,1)S(1)}, bf16[320,256]{1,0:T(8,128)(2,1)S(1)}, u32[]{:S(2)}, u32[]{:S(2)}) collective-permute-start(bf16[320,256]{1,0:T(8,128)(2,1)S(1)} %get-tuple-element.63), channel_id=1, source_target_pairs={{0,4},{4,8},{8,12},{12,0},{1,5},{5,9},{9,13},{13,1},{2,6},{6,10},{... | collective-permute-start | bytes 491528 | tf_op jit(solution)/shard_map/ppermute | solution.py:247
  10.3 1.2 %collective-permute-start.3 = (bf16[320,256]{1,0:T(8,128)(2,1)S(1)}, bf16[320,256]{1,0:T(8,128)(2,1)S(1)}, u32[]{:S(2)}, u32[]{:S(2)}) collective-permute-start(bf16[320,256]{1,0:T(8,128)(2,1)S(1)} %get-tuple-element.65), channel_id=1, source_target_pairs={{0,8},{4,12},{8,0},{12,4},{1,9},{5,13},{9,1},{13,5},{2,10},{6,14},... | collective-permute-start | bytes 491528 | tf_op jit(solution)/shard_map/ppermute | solution.py:247
  11.5 2.7 %collective-permute-start.4 = (bf16[320,256]{1,0:T(8,128)(2,1)S(1)}, bf16[320,256]{1,0:T(8,128)(2,1)S(1)}, u32[]{:S(2)}, u32[]{:S(2)}) collective-permute-start(bf16[320,256]{1,0:T(8,128)(2,1)S(1)} %get-tuple-element.66), channel_id=1, source_target_pairs={{0,12},{4,0},{8,4},{12,8},{1,13},{5,1},{9,5},{13,9},{2,14},{6,2},{... | collective-permute-start | bytes 491528 | tf_op jit(solution)/shard_map/ppermute | solution.py:247
  14.2 1.0 %spread_modes.1 = (bf16[256,256]{1,0:T(8,128)(2,1)S(1)}, bf16[256,256]{1,0:T(8,128)(2,1)S(1)}, f32[640,256]{1,0:T(8,128)S(1)}) custom-call(s32[4]{0:T(128)S(1)} %pad_add_fusion.refs_0_, bf16[128,128]{1,0:T(8,128)(2,1)S(1)} %copy-done.1, bf16[128,128]{1,0:T(8,128)(2,1)S(1)} %copy-done.2, f32[1,128]{1,0:T(1,128)S(1)} %bitcast.9, ...), custom_call_target="tpu_custom_call" | custom-call | flops 25165824 | tf_op jit(solution)/shard_map/spread_modes/pallas_call | solution.py:41
  15.3 1.6 %split_table.2 = (bf16[320,1280]{1,0:T(8,128)(2,1)S(1)}, bf16[320,1280]{1,0:T(8,128)(2,1)S(1)}) custom-call(s32[4]{0:T(128)S(1)} %pad_add_fusion.refs_0_, bf16[320,1280]{1,0:T(8,128)(2,1)S(1)} %bitcast.12, bf16[320,1280]{1,0:T(8,128)(2,1)S(1)} %collective-permute-done.refs_2_), custom_call_target="tpu_custom_call" | custom-call | flops 524288000 | tf_op jit(solution)/shard_map/split_table/pallas_call | solution.py:41
  16.8 2.8 %collective-permute-done.2.refs_2_ = bf16[320,256]{1,0:T(8,128)(2,1)S(1)} collective-permute-done((bf16[320,256]{1,0:T(8,128)(2,1)S(1)}, bf16[320,256]{1,0:T(8,128)(2,1)S(1)}, u32[]{:S(2)}, u32[]{:S(2)}) %collective-permute-start.2) | collective-permute-done | bytes 163872 | tf_op jit(solution)/shard_map/ppermute | solution.py:247
  19.6 6.3 %collective-permute-done.3.refs_3_ = bf16[320,256]{1,0:T(8,128)(2,1)S(1)} collective-permute-done((bf16[320,256]{1,0:T(8,128)(2,1)S(1)}, bf16[320,256]{1,0:T(8,128)(2,1)S(1)}, u32[]{:S(2)}, u32[]{:S(2)}) %collective-permute-start.3) | collective-permute-done | bytes 163872 | tf_op jit(solution)/shard_map/ppermute | solution.py:247
  25.9 0.0 collective-permute-done.4.refs_4_
  25.9 1.0 %direct_legendre_near.2 = (bf16[320,256]{1,0:T(8,128)(2,1)S(1)}, bf16[1280,256]{1,0:T(8,128)(2,1)S(1)}) custom-call(s32[4]{0:T(128)S(1)} %pad_add_fusion.refs_0_, bf16[320,256]{1,0:T(8,128)(2,1)S(1)} %get-tuple-element.61.refs_4_.refs_1_, bf16[320,256]{1,0:T(8,128)(2,1)S(1)} %collective-permute-done.1.refs_2_, ...), custom_call_target="tpu_custom_call" | custom-call | flops 209715200 | tf_op jit(solution)/shard_map/direct_legendre_near/pallas_call | solution.py:41
  26.9 0.0 collective-permute-done.5.refs_1_
  26.9 0.1 collective-permute-start.6
  27.0 3.0 %collective-permute-start.8 = (bf16[320,256]{1,0:T(8,128)(2,1)S(1)}, bf16[320,256]{1,0:T(8,128)(2,1)S(1)}, u32[]{:S(2)}, u32[]{:S(2)}) collective-permute-start(bf16[320,256]{1,0:T(8,128)(2,1)S(1)} %get-tuple-element.75), channel_id=1, source_target_pairs={{0,8},{4,12},{8,0},{12,4},{1,9},{5,13},{9,1},{13,5},{2,10},{6,14},... | collective-permute-start | bytes 491528 | tf_op jit(solution)/shard_map/ppermute | solution.py:247
  30.0 0.5 collective-permute-start.7
  30.5 7.8 %collective-permute-done.8.refs_3_ = bf16[320,256]{1,0:T(8,128)(2,1)S(1)} collective-permute-done((bf16[320,256]{1,0:T(8,128)(2,1)S(1)}, bf16[320,256]{1,0:T(8,128)(2,1)S(1)}, u32[]{:S(2)}, u32[]{:S(2)}) %collective-permute-start.8) | collective-permute-done | bytes 163872 | tf_op jit(solution)/shard_map/ppermute | solution.py:247
  38.3 1.6 %split_table.3 = (bf16[320,1280]{1,0:T(8,128)(2,1)S(1)}, bf16[320,1280]{1,0:T(8,128)(2,1)S(1)}) custom-call(s32[4]{0:T(128)S(1)} %pad_add_fusion.refs_0_, bf16[320,1280]{1,0:T(8,128)(2,1)S(1)} %collective-permute-done.5.refs_1_, bf16[320,1280]{1,0:T(8,128)(2,1)S(1)} %collective-permute-done.6.refs_2_), custom_call_target="tpu_custom_call" | custom-call | flops 524288000 | tf_op jit(solution)/shard_map/split_table/pallas_call | solution.py:41
  39.9 0.4 direct_legendre_far.2.refs_0_
  40.3 0.4 vertical_solve.2
  40.7 0.6 collective-permute-start.9
  41.3 3.6 %collective-permute-start.10 = (bf16[320,256]{1,0:T(8,128)(2,1)S(1)}, bf16[320,256]{1,0:T(8,128)(2,1)S(1)}, u32[]{:S(2)}, u32[]{:S(2)}) collective-permute-start(bf16[320,256]{1,0:T(8,128)(2,1)S(1)} %get-tuple-element.85), channel_id=1, source_target_pairs={{0,12},{4,0},{8,4},{12,8},{1,13},{5,1},{9,5},{13,9},{2,14},{6,2},{... | collective-permute-start | bytes 491528 | tf_op jit(solution)/shard_map/ppermute | solution.py:247
  44.9 0.5 inverse_legendre_far.2.refs_1_
  45.4 1.3 %collective-permute-done.9.refs_2_.refs_1_ = bf16[320,256]{1,0:T(8,128)(2,1)S(1)} collective-permute-done((bf16[320,256]{1,0:T(8,128)(2,1)S(1)}, bf16[320,256]{1,0:T(8,128)(2,1)S(1)}, u32[]{:S(2)}, u32[]{:S(2)}) %collective-permute-start.9) | collective-permute-done | bytes 163872 | tf_op jit(solution)/shard_map/ppermute | solution.py:247
  46.7 1.2 %inverse_legendre_near.2 = (bf16[320,256]{1,0:T(8,128)(2,1)S(1)}, bf16[320,256]{1,0:T(8,128)(2,1)S(1)}, bf16[320,256]{1,0:T(8,128)(2,1)S(1)}, bf16[320,256]{1,0:T(8,128)(2,1)S(1)}) custom-call(s32[4]{0:T(128)S(1)} %pad_add_fusion.refs_0_, f32[1280,256]{1,0:T(8,128)S(1)} %inverse_legendre_far.2.refs_1_, ...), custom_call_target="tpu_custom_call" | custom-call | flops 209715200 | tf_op jit(solution)/shard_map/inverse_legendre_near/pallas_call | solution.py:41
  47.9 0.4 collective-permute-done.10.refs_4_
  48.3 1.0 %direct_legendre_near.3 = (bf16[320,256]{1,0:T(8,128)(2,1)S(1)}, bf16[1280,256]{1,0:T(8,128)(2,1)S(1)}) custom-call(s32[4]{0:T(128)S(1)} %pad_add_fusion.refs_0_, bf16[320,256]{1,0:T(8,128)(2,1)S(1)} %get-tuple-element.82.refs_1_, bf16[320,256]{1,0:T(8,128)(2,1)S(1)} %collective-permute-done.2.refs_2_, bf16[320,256]{1,0:T(8,128)(2,1)S(1)} %collective-permute-done.8.refs_3_, ...), custom_call_target="tpu_custom_call" | custom-call | flops 209715200 | tf_op jit(solution)/shard_map/direct_legendre_near/pallas_call | solution.py:41
  49.2 1.6 %collective-permute-start.11 = (bf16[320,256]{1,0:T(8,128)(2,1)S(1)}, bf16[320,256]{1,0:T(8,128)(2,1)S(1)}, u32[]{:S(2)}, u32[]{:S(2)}) collective-permute-start(bf16[320,256]{1,0:T(8,128)(2,1)S(1)} %get-tuple-element.87), channel_id=1, source_target_pairs={{0,2},{2,0},{1,3},{3,1},{4,6},{6,4},{5,7},{7,5},{8,10},{10,8},{9,1... | collective-permute-start | bytes 491528 | tf_op jit(solution)/shard_map/ppermute | solution.py:247
  50.8 4.8 %collective-permute-start.14 = (bf16[320,256]{1,0:T(8,128)(2,1)S(1)}, bf16[320,256]{1,0:T(8,128)(2,1)S(1)}, u32[]{:S(2)}, u32[]{:S(2)}) collective-permute-start(bf16[320,256]{1,0:T(8,128)(2,1)S(1)} %get-tuple-element.94), channel_id=1, source_target_pairs={{0,8},{4,12},{8,0},{12,4},{1,9},{5,13},{9,1},{13,5},{2,10},{6,14},... | collective-permute-start | bytes 491528 | tf_op jit(solution)/shard_map/ppermute | solution.py:247
  55.7 0.4 direct_legendre_far.3.refs_0_
  56.1 4.2 %collective-permute-done.12.refs_2_ = bf16[320,256]{1,0:T(8,128)(2,1)S(1)} collective-permute-done((bf16[320,256]{1,0:T(8,128)(2,1)S(1)}, bf16[320,256]{1,0:T(8,128)(2,1)S(1)}, u32[]{:S(2)}, u32[]{:S(2)}) %collective-permute-start.12) | collective-permute-done | bytes 163872 | tf_op jit(solution)/shard_map/ppermute | solution.py:247
  60.3 0.4 vertical_solve.3
  60.7 0.6 collective-permute-start.13
  61.3 0.5 inverse_legendre_far.3.refs_1_
  61.9 3.3 %collective-permute-done.14.refs_3_ = bf16[320,256]{1,0:T(8,128)(2,1)S(1)} collective-permute-done((bf16[320,256]{1,0:T(8,128)(2,1)S(1)}, bf16[320,256]{1,0:T(8,128)(2,1)S(1)}, u32[]{:S(2)}, u32[]{:S(2)}) %collective-permute-start.14) | collective-permute-done | bytes 163872 | tf_op jit(solution)/shard_map/ppermute | solution.py:247
  65.2 0.9 %collective-permute-done.13.refs_2_.refs_3_ = bf16[320,256]{1,0:T(8,128)(2,1)S(1)} collective-permute-done((bf16[320,256]{1,0:T(8,128)(2,1)S(1)}, bf16[320,256]{1,0:T(8,128)(2,1)S(1)}, u32[]{:S(2)}, u32[]{:S(2)}) %collective-permute-start.13) | collective-permute-done | bytes 163872 | tf_op jit(solution)/shard_map/ppermute | solution.py:247
  66.1 1.2 %inverse_legendre_near.3 = (bf16[320,256]{1,0:T(8,128)(2,1)S(1)}, bf16[320,256]{1,0:T(8,128)(2,1)S(1)}, bf16[320,256]{1,0:T(8,128)(2,1)S(1)}, bf16[320,256]{1,0:T(8,128)(2,1)S(1)}) custom-call(s32[4]{0:T(128)S(1)} %pad_add_fusion.refs_0_, f32[1280,256]{1,0:T(8,128)S(1)} %inverse_legendre_far.3.refs_1_, ...), custom_call_target="tpu_custom_call" | custom-call | flops 209715200 | tf_op jit(solution)/shard_map/inverse_legendre_near/pallas_call | solution.py:41
  67.3 3.5 %collective-permute-start.16 = (bf16[320,256]{1,0:T(8,128)(2,1)S(1)}, bf16[320,256]{1,0:T(8,128)(2,1)S(1)}, u32[]{:S(2)}, u32[]{:S(2)}) collective-permute-start(bf16[320,256]{1,0:T(8,128)(2,1)S(1)} %get-tuple-element.101), channel_id=1, source_target_pairs={{0,4},{4,8},{8,12},{12,0},{1,5},{5,9},{9,13},{13,1},{2,6},{6,10},{... | collective-permute-start | bytes 491528 | tf_op jit(solution)/shard_map/ppermute | solution.py:247
  70.8 2.0 %collective-permute-start.17 = (bf16[320,256]{1,0:T(8,128)(2,1)S(1)}, bf16[320,256]{1,0:T(8,128)(2,1)S(1)}, u32[]{:S(2)}, u32[]{:S(2)}) collective-permute-start(bf16[320,256]{1,0:T(8,128)(2,1)S(1)} %get-tuple-element.102), channel_id=1, source_target_pairs={{0,8},{4,12},{8,0},{12,4},{1,9},{5,13},{9,1},{13,5},{2,10},{6,14},... | collective-permute-start | bytes 491528 | tf_op jit(solution)/shard_map/ppermute | solution.py:247
  72.8 2.8 %collective-permute-start.18 = (bf16[320,256]{1,0:T(8,128)(2,1)S(1)}, bf16[320,256]{1,0:T(8,128)(2,1)S(1)}, u32[]{:S(2)}, u32[]{:S(2)}) collective-permute-start(bf16[320,256]{1,0:T(8,128)(2,1)S(1)} %get-tuple-element.103), channel_id=1, source_target_pairs={{0,12},{4,0},{8,4},{12,8},{1,13},{5,1},{9,5},{13,9},{2,14},{6,2},{... | collective-permute-start | bytes 491528 | tf_op jit(solution)/shard_map/ppermute | solution.py:247
  75.6 1.7 %order_spectral.1 = bf16[2560,128]{1,0:T(8,128)(2,1)} custom-call(s32[4]{0:T(128)S(1)} %pad_add_fusion.refs_0_, bf16[320,256]{1,0:T(8,128)(2,1)S(1)} %collective-permute-done.9.refs_2_.refs_1_, bf16[320,256]{1,0:T(8,128)(2,1)S(1)} %get-tuple-element.79.refs_0_.refs_2_, bf16[320,256]{1,0:T(8,128)(2,1)S(1)} %collective-permute-done.13.refs_2_.refs_3_, ...), custom_call_target="tpu_custom_call" | custom-call | tf_op jit(solution)/shard_map/order_spectral/pallas_call | solution.py:41
  77.4 4.2 %collective-permute-done.17.refs_7_ = bf16[320,256]{1,0:T(8,128)(2,1)S(1)} collective-permute-done((bf16[320,256]{1,0:T(8,128)(2,1)S(1)}, bf16[320,256]{1,0:T(8,128)(2,1)S(1)}, u32[]{:S(2)}, u32[]{:S(2)}) %collective-permute-start.17) | collective-permute-done | bytes 163872 | tf_op jit(solution)/shard_map/ppermute | solution.py:247
  81.6 2.1 %join_hemispheres.1 = bf16[2,2560,128]{2,1,0:T(8,128)(2,1)} custom-call(s32[4]{0:T(128)S(1)} %pad_add_fusion.refs_0_, bf16[320,256]{1,0:T(8,128)(2,1)S(1)} %get-tuple-element.81.refs_6_.refs_1_, bf16[320,256]{1,0:T(8,128)(2,1)S(1)} %collective-permute-done.12.refs_2_, bf16[320,256]{1,0:T(8,128)(2,1)S(1)} %collective-permute-done.14.refs_3_, ...), custom_call_target="tpu_custom_call" | custom-call | flops 335544320 | tf_op jit(solution)/shard_map/join_hemispheres/pallas_call | solution.py:41
  (19 shorter events, 0.1 us)
Async XLA Ops:
  0.6 13.6 %copy-start.3 = (f32[128]{0:T(128)S(1)}, f32[128]{0:T(128)}, u32[]{:S(2)}) copy-start(f32[128]{0:T(128)} %param.11) | copy-start | bytes 1540
  0.6 13.6 %copy-start.2 = (bf16[128,128]{1,0:T(8,128)(2,1)S(1)}, bf16[128,128]{1,0:T(8,128)(2,1)}, u32[]{:S(2)}) copy-start(bf16[128,128]{1,0:T(8,128)(2,1)} %refs_2_.1) | copy-start | bytes 98308
  0.7 13.5 %copy-start.1 = (bf16[128,128]{1,0:T(8,128)(2,1)S(1)}, bf16[128,128]{1,0:T(8,128)(2,1)}, u32[]{:S(2)}) copy-start(bf16[128,128]{1,0:T(8,128)(2,1)} %refs_1_.1) | copy-start | bytes 98308
  0.7 6.4 %collective-permute-start = (bf16[320,1280]{1,0:T(8,128)(2,1)}, bf16[320,1280]{1,0:T(8,128)(2,1)S(1)}, u32[]{:S(2)}, u32[]{:S(2)}) collective-permute-start(bf16[320,1280]{1,0:T(8,128)(2,1)} %bitcast.10), channel_id=1, source_target_pairs={{0,1},{1,0},{2,3},{3,2},{4,5},{5,4},{6,7},{7,6},{8,9},{9,8},{10,11... | collective-permute-start | bytes 2457608 | tf_op jit(solution)/shard_map/ppermute | solution.py:247
  1.2 25.7 %collective-permute-start.5 = (bf16[320,1280]{1,0:T(8,128)(2,1)}, bf16[320,1280]{1,0:T(8,128)(2,1)S(1)}, u32[]{:S(2)}, u32[]{:S(2)}) collective-permute-start(bf16[320,1280]{1,0:T(8,128)(2,1)} %bitcast.11), channel_id=1, source_target_pairs={{0,2},{2,0},{1,3},{3,1},{4,6},{6,4},{5,7},{7,5},{8,10},{10,8},{9,1... | collective-permute-start | bytes 2457608 | tf_op jit(solution)/shard_map/ppermute | solution.py:247
  4.6 1.3 %copy-start = (bf16[2,320,4,2,128]{4,3,2,1,0:T(2,128)(2,1)S(1)}, bf16[2,320,4,2,128]{4,3,2,1,0:T(2,128)(2,1)}, u32[]{:S(2)}) copy-start(bf16[2,320,4,2,128]{4,3,2,1,0:T(2,128)(2,1)} %param.6) | copy-start | bytes 3932164
  6.0 9.3 %copy-start.4 = (bf16[1,320,1280]{2,1,0:T(8,128)(2,1)S(1)}, bf16[1,320,1280]{2,1,0:T(8,128)(2,1)}, u32[]{:S(2)}) copy-start(bf16[1,320,1280]{2,1,0:T(8,128)(2,1)} %param.7) | copy-start | bytes 2457604
  7.0 9.8 %collective-permute-start.1 = (bf16[320,256]{1,0:T(8,128)(2,1)S(1)}, bf16[320,256]{1,0:T(8,128)(2,1)S(1)}, u32[]{:S(2)}, u32[]{:S(2)}) collective-permute-start(bf16[320,256]{1,0:T(8,128)(2,1)S(1)} %get-tuple-element.62), channel_id=1, source_target_pairs={{0,4},{4,8},{8,12},{12,0},{1,5},{5,9},{9,13},{13,1},{2,6},{6,10},{... | collective-permute-start | bytes 491528 | tf_op jit(solution)/shard_map/ppermute | solution.py:247
  8.7 10.9 %collective-permute-start.2 = (bf16[320,256]{1,0:T(8,128)(2,1)S(1)}, bf16[320,256]{1,0:T(8,128)(2,1)S(1)}, u32[]{:S(2)}, u32[]{:S(2)}) collective-permute-start(bf16[320,256]{1,0:T(8,128)(2,1)S(1)} %get-tuple-element.63), channel_id=1, source_target_pairs={{0,4},{4,8},{8,12},{12,0},{1,5},{5,9},{9,13},{13,1},{2,6},{6,10},{... | collective-permute-start | bytes 491528 | tf_op jit(solution)/shard_map/ppermute | solution.py:247
  10.3 15.6 %collective-permute-start.3 = (bf16[320,256]{1,0:T(8,128)(2,1)S(1)}, bf16[320,256]{1,0:T(8,128)(2,1)S(1)}, u32[]{:S(2)}, u32[]{:S(2)}) collective-permute-start(bf16[320,256]{1,0:T(8,128)(2,1)S(1)} %get-tuple-element.65), channel_id=1, source_target_pairs={{0,8},{4,12},{8,0},{12,4},{1,9},{5,13},{9,1},{13,5},{2,10},{6,14},... | collective-permute-start | bytes 491528 | tf_op jit(solution)/shard_map/ppermute | solution.py:247
  11.5 14.4 %collective-permute-start.4 = (bf16[320,256]{1,0:T(8,128)(2,1)S(1)}, bf16[320,256]{1,0:T(8,128)(2,1)S(1)}, u32[]{:S(2)}, u32[]{:S(2)}) collective-permute-start(bf16[320,256]{1,0:T(8,128)(2,1)S(1)} %get-tuple-element.66), channel_id=1, source_target_pairs={{0,12},{4,0},{8,4},{12,8},{1,13},{5,1},{9,5},{13,9},{2,14},{6,2},{... | collective-permute-start | bytes 491528 | tf_op jit(solution)/shard_map/ppermute | solution.py:247
  26.9 11.4 %collective-permute-start.6 = (bf16[320,1280]{1,0:T(8,128)(2,1)S(1)}, bf16[320,1280]{1,0:T(8,128)(2,1)S(1)}, u32[]{:S(2)}, u32[]{:S(2)}) collective-permute-start(bf16[320,1280]{1,0:T(8,128)(2,1)S(1)} %collective-permute-done.5.refs_1_), channel_id=1, source_target_pairs={{0,1},{1,0},{2,3},{3,2},{4,5},{5,4},{6,7},{7,6},{8,9},{9,8},{10,11... | collective-permute-start | bytes 2457608 | tf_op jit(solution)/shard_map/ppermute | solution.py:247
  27.0 11.3 %collective-permute-start.8 = (bf16[320,256]{1,0:T(8,128)(2,1)S(1)}, bf16[320,256]{1,0:T(8,128)(2,1)S(1)}, u32[]{:S(2)}, u32[]{:S(2)}) collective-permute-start(bf16[320,256]{1,0:T(8,128)(2,1)S(1)} %get-tuple-element.75), channel_id=1, source_target_pairs={{0,8},{4,12},{8,0},{12,4},{1,9},{5,13},{9,1},{13,5},{2,10},{6,14},... | collective-permute-start | bytes 491528 | tf_op jit(solution)/shard_map/ppermute | solution.py:247
  30.0 8.3 %collective-permute-start.7 = (bf16[320,256]{1,0:T(8,128)(2,1)S(1)}, bf16[320,256]{1,0:T(8,128)(2,1)S(1)}, u32[]{:S(2)}, u32[]{:S(2)}) collective-permute-start(bf16[320,256]{1,0:T(8,128)(2,1)S(1)} %get-tuple-element.74), channel_id=1, source_target_pairs={{0,2},{2,0},{1,3},{3,1},{4,6},{6,4},{5,7},{7,5},{8,10},{10,8},{9,1... | collective-permute-start | bytes 491528 | tf_op jit(solution)/shard_map/ppermute | solution.py:247
  40.7 6.0 %collective-permute-start.9 = (bf16[320,256]{1,0:T(8,128)(2,1)S(1)}, bf16[320,256]{1,0:T(8,128)(2,1)S(1)}, u32[]{:S(2)}, u32[]{:S(2)}) collective-permute-start(bf16[320,256]{1,0:T(8,128)(2,1)S(1)} %get-tuple-element.80), channel_id=1, source_target_pairs={{0,2},{2,0},{1,3},{3,1},{4,6},{6,4},{5,7},{7,5},{8,10},{10,8},{9,1... | collective-permute-start | bytes 491528 | tf_op jit(solution)/shard_map/ppermute | solution.py:247
  41.3 7.0 %collective-permute-start.10 = (bf16[320,256]{1,0:T(8,128)(2,1)S(1)}, bf16[320,256]{1,0:T(8,128)(2,1)S(1)}, u32[]{:S(2)}, u32[]{:S(2)}) collective-permute-start(bf16[320,256]{1,0:T(8,128)(2,1)S(1)} %get-tuple-element.85), channel_id=1, source_target_pairs={{0,12},{4,0},{8,4},{12,8},{1,13},{5,1},{9,5},{13,9},{2,14},{6,2},{... | collective-permute-start | bytes 491528 | tf_op jit(solution)/shard_map/ppermute | solution.py:247
  49.2 6.8 %collective-permute-start.11 = (bf16[320,256]{1,0:T(8,128)(2,1)S(1)}, bf16[320,256]{1,0:T(8,128)(2,1)S(1)}, u32[]{:S(2)}, u32[]{:S(2)}) collective-permute-start(bf16[320,256]{1,0:T(8,128)(2,1)S(1)} %get-tuple-element.87), channel_id=1, source_target_pairs={{0,2},{2,0},{1,3},{3,1},{4,6},{6,4},{5,7},{7,5},{8,10},{10,8},{9,1... | collective-permute-start | bytes 491528 | tf_op jit(solution)/shard_map/ppermute | solution.py:247
  50.8 9.5 %collective-permute-start.12 = (bf16[320,256]{1,0:T(8,128)(2,1)S(1)}, bf16[320,256]{1,0:T(8,128)(2,1)S(1)}, u32[]{:S(2)}, u32[]{:S(2)}) collective-permute-start(bf16[320,256]{1,0:T(8,128)(2,1)S(1)} %get-tuple-element.88), channel_id=1, source_target_pairs={{0,4},{4,8},{8,12},{12,0},{1,5},{5,9},{9,13},{13,1},{2,6},{6,10},{... | collective-permute-start | bytes 491528 | tf_op jit(solution)/shard_map/ppermute | solution.py:247
  50.8 14.4 %collective-permute-start.14 = (bf16[320,256]{1,0:T(8,128)(2,1)S(1)}, bf16[320,256]{1,0:T(8,128)(2,1)S(1)}, u32[]{:S(2)}, u32[]{:S(2)}) collective-permute-start(bf16[320,256]{1,0:T(8,128)(2,1)S(1)} %get-tuple-element.94), channel_id=1, source_target_pairs={{0,8},{4,12},{8,0},{12,4},{1,9},{5,13},{9,1},{13,5},{2,10},{6,14},... | collective-permute-start | bytes 491528 | tf_op jit(solution)/shard_map/ppermute | solution.py:247
  55.7 9.5 %collective-permute-start.15 = (bf16[320,256]{1,0:T(8,128)(2,1)S(1)}, bf16[320,256]{1,0:T(8,128)(2,1)S(1)}, u32[]{:S(2)}, u32[]{:S(2)}) collective-permute-start(bf16[320,256]{1,0:T(8,128)(2,1)S(1)} %get-tuple-element.95), channel_id=1, source_target_pairs={{0,12},{4,0},{8,4},{12,8},{1,13},{5,1},{9,5},{13,9},{2,14},{6,2},{... | collective-permute-start | bytes 491528 | tf_op jit(solution)/shard_map/ppermute | solution.py:247
  60.7 5.4 %collective-permute-start.13 = (bf16[320,256]{1,0:T(8,128)(2,1)S(1)}, bf16[320,256]{1,0:T(8,128)(2,1)S(1)}, u32[]{:S(2)}, u32[]{:S(2)}) collective-permute-start(bf16[320,256]{1,0:T(8,128)(2,1)S(1)} %get-tuple-element.93), channel_id=1, source_target_pairs={{0,2},{2,0},{1,3},{3,1},{4,6},{6,4},{5,7},{7,5},{8,10},{10,8},{9,1... | collective-permute-start | bytes 491528 | tf_op jit(solution)/shard_map/ppermute | solution.py:247
  67.3 10.1 %collective-permute-start.16 = (bf16[320,256]{1,0:T(8,128)(2,1)S(1)}, bf16[320,256]{1,0:T(8,128)(2,1)S(1)}, u32[]{:S(2)}, u32[]{:S(2)}) collective-permute-start(bf16[320,256]{1,0:T(8,128)(2,1)S(1)} %get-tuple-element.101), channel_id=1, source_target_pairs={{0,4},{4,8},{8,12},{12,0},{1,5},{5,9},{9,13},{13,1},{2,6},{6,10},{... | collective-permute-start | bytes 491528 | tf_op jit(solution)/shard_map/ppermute | solution.py:247
  70.8 10.8 %collective-permute-start.17 = (bf16[320,256]{1,0:T(8,128)(2,1)S(1)}, bf16[320,256]{1,0:T(8,128)(2,1)S(1)}, u32[]{:S(2)}, u32[]{:S(2)}) collective-permute-start(bf16[320,256]{1,0:T(8,128)(2,1)S(1)} %get-tuple-element.102), channel_id=1, source_target_pairs={{0,8},{4,12},{8,0},{12,4},{1,9},{5,13},{9,1},{13,5},{2,10},{6,14},... | collective-permute-start | bytes 491528 | tf_op jit(solution)/shard_map/ppermute | solution.py:247
  72.8 8.8 %collective-permute-start.18 = (bf16[320,256]{1,0:T(8,128)(2,1)S(1)}, bf16[320,256]{1,0:T(8,128)(2,1)S(1)}, u32[]{:S(2)}, u32[]{:S(2)}) collective-permute-start(bf16[320,256]{1,0:T(8,128)(2,1)S(1)} %get-tuple-element.103), channel_id=1, source_target_pairs={{0,12},{4,0},{8,4},{12,8},{1,13},{5,1},{9,5},{13,9},{2,14},{6,2},{... | collective-permute-start | bytes 491528 | tf_op jit(solution)/shard_map/ppermute | solution.py:247
